TPU v7x, 512 devices: a whole 4x8x8 slice. The times are simulated.
512 devices in a mesh: section: 8 (over y), dp: 4 (over x_lo, core), tensor: 16 (over x_hi, z).
Axes of the slice: x: 4 (x_hi: 2, x_lo: 2; x = x_hi * 2 + x_lo), y: 8, z: 8, core: 2. Of those that a mesh axis runs over, the one named last changes fastest.
Arguments:
- train_act: bfloat16 [8, 4096, 5120], P('section', ('dp', 'tensor')), may hold values from -0.75 to 0.75
- train_grad: bfloat16 [8, 4096, 27648], P('section', 'dp', 'tensor'), may hold values from -0.5 to 0.5
- val_act: bfloat16 [8, 512, 5120], P('section', ('dp', 'tensor')), may hold values from -0.75 to 0.75
- val_grad: bfloat16 [8, 512, 27648], P('section', 'dp', 'tensor'), may hold values from -0.5 to 0.5
- segment_ids: int32 [4, 1024], P('dp'), may hold values from 0 to 3, never falling along the last dimension, each value on 1 to 512 neighbouring positions
- val_lengths: int32 [8], replicated, may hold values from 1 to 64, 384 in all
Outputs:
- scores: float32 [4, 4], P('dp')
Inputs may be any that keep to these rules, and one draw needn't show every extreme that they name: `segment_ids`: ids never fall along a row, each of the 4 ids holds 1 to 512 tokens of every row, and one holds exactly that many. `val_lengths`: the lengths sum to 384 and the largest is exactly 64.
All inputs are finite; a program needn't handle non-finite values.
Results may differ from a plain program's by a relative error of at most 0.0003.
Values may be sent and summed in bfloat16 or wider, within the bound.
No kernel may reach another device: no remote copies, remote signals or barrier semaphores. Data moves between devices by JAX's collectives and lax.ppermute only.
A program may use at most 64 MiB of HBM per device.

v0:
```python
import jax
import jax.numpy as jnp
from jax import lax
from jax.sharding import PartitionSpec as P

SEQ_DEV = 4
VSEQ = 8
VLEN = 64


def rows_gram(left, right):
    dims = (((1,), (1,)), ((), ()))
    return lax.dot_general(left, right, dims, preferred_element_type=jnp.float32)


def on_device(train_act, train_grad, val_act, val_grad, segment_ids, val_lengths):
    act_rows = train_act[0]
    grad_rows = train_grad[0]
    tok_count = segment_ids.shape[1]
    positions = jnp.arange(VLEN, dtype=jnp.int32)
    live = (positions[None, :] < val_lengths[:, None]).astype(jnp.float32).reshape(VSEQ * VLEN)
    val_grads = lax.all_gather(val_grad[0], "dp", axis=0, tiled=True)
    val_acts = lax.all_gather(val_act[0], ("dp", "tensor"), axis=0, tiled=True)
    act_gram = rows_gram(act_rows, val_acts)
    seq_numbers = jnp.arange(SEQ_DEV, dtype=jnp.int32)[:, None]
    grad_total = lax.psum(rows_gram(grad_rows, val_grads), "tensor")
    act_all = lax.all_gather(act_gram, "tensor", axis=0, tiled=True)
    per_token = jnp.dot(act_all * grad_total, live, precision=lax.Precision.HIGHEST)
    onehot = (segment_ids[0][None, :] == seq_numbers).astype(jnp.float32)
    local_terms = jnp.dot(onehot, per_token, precision=lax.Precision.HIGHEST)
    totals = lax.psum(local_terms, "section")
    norm_factor = jnp.sqrt(jnp.float32(tok_count * VSEQ * VLEN * lax.axis_size("section")))
    return (totals / norm_factor)[None, :]


def solution(mesh):
    placed = (
        P("section", ("dp", "tensor"), None),
        P("section", "dp", "tensor"),
        P("section", ("dp", "tensor"), None),
        P("section", "dp", "tensor"),
        P("dp", None),
        P(),
    )
    return jax.shard_map(
        on_device, mesh=mesh, in_specs=placed, out_specs=P("dp", None), check_vma=False
    )
```

profile of v0, /device:TPU:1, one launch (start us, length us, event | category | flops | bytes accessed | tf_op | source)
XLA Modules:
  0.0 528.7 jit_solution(7529640914884658881)
XLA Ops:
  6.5 0.0 copy-start
  6.5 0.0 all-gather.10.cloned.1.call-start
  6.5 0.7 all-gather.10.cloned.1.call-update
  7.3 0.0 all-gather.8.cloned.1.call-start
  7.3 0.7 all-gather.8.cloned.1.call-update
  8.0 0.0 all-reduce.2.cloned.1.call-start
  8.1 39.0 %all-gather.10.cloned.1.call-done = bf16[1,512,1728]{1,2,0:T(8,128)(2,1)} async-done(((bf16[1,128,1728]{1,2,0:T(8,128)(2,1)}), bf16[1,512,1728]{1,2,0:T(8,128)(2,1)}) %all-gather.10.cloned.1.call-update) | async-done | bytes 1769488 | tf_op jit(solution)/shard_map/all_gather | solution.py:22
  47.0 0.0 copy-done
  47.0 5.0 fusion.2
  52.0 0.0 all-reduce.2.cloned.1.call-update
  52.0 0.0 copy-start.2
  52.0 0.0 all-gather.6.cloned.1.call-start
  52.1 188.1 %all-gather.8.cloned.1.call-done = bf16[1,512,5120]{2,1,0:T(8,128)(2,1)} async-done(((bf16[1,8,5120]{2,1,0:T(8,128)(2,1)}), bf16[1,512,5120]{2,1,0:T(8,128)(2,1)}) %all-gather.8.cloned.1.call-update) | async-done | bytes 5242896 | tf_op jit(solution)/shard_map/all_gather | solution.py:23
  240.2 5.1 fusion
  245.2 0.0 all-gather.6.cloned.1.call-update
  245.3 0.0 copy-done.2
  245.3 0.1 iota_compare_fusion.2
  245.4 0.1 reshape.7
  245.4 0.0 copy-start.1
  245.4 160.9 %all-reduce.2.cloned.1.call-done = f32[1024,512]{1,0:T(8,128)} async-done(((f32[1024,512]{1,0:T(8,128)}), f32[1024,512]{1,0:T(8,128)}) %all-reduce.2.cloned.1.call-update) | async-done | bytes 2097168 | tf_op jit(solution)/shard_map/psum | solution.py:26
  406.4 98.4 %all-gather.6.cloned.1.call-done = f32[1024,512]{1,0:T(8,128)} async-done(((f32[64,512]{1,0:T(8,128)}), f32[1024,512]{1,0:T(8,128)}) %all-gather.6.cloned.1.call-update) | async-done | bytes 2097168 | tf_op jit(solution)/shard_map/all_gather | solution.py:27
  504.8 3.3 fusion.7
  508.1 0.0 copy-done.1
  508.1 0.1 convolution_bitcast_fusion
  508.2 13.4 %psum.15 = f32[4]{0:T(128)S(1)} all-reduce(f32[4]{0:T(128)S(1)} %convolution_bitcast_fusion), channel_id=1, replica_groups=mesh['section'=8,'dp'=4,'tensor'=16] {'section'}, use_global_device_ids=true, to_apply=%region_1.0 | all-reduce | flops 4 | bytes 32 | tf_op jit(solution)/shard_map/psum | solution.py:31
  521.6 0.5 multiply_bitcast_fusion
Async XLA Ops:
  6.5 40.5 %copy-start = (bf16[1,1024,1728]{1,2,0:T(8,128)(2,1)S(1)}, bf16[1,1024,1728]{1,2,0:T(8,128)(2,1)}, u32[]{:S(2)}) copy-start(bf16[1,1024,1728]{1,2,0:T(8,128)(2,1)} %param.7) | copy-start | bytes 10616836
  6.5 40.5 %all-gather.10.cloned.1.call-start = ((), (), s32[]{:S(2)}) async-start(), calls=%async_computation.3 | async-start | bytes 2211840 | tf_op jit(solution)/shard_map/all_gather | solution.py:22
  7.3 232.9 %all-gather.8.cloned.1.call-start = ((), (), s32[]{:S(2)}) async-start(), calls=%async_computation.2 | async-start | bytes 5324800 | tf_op jit(solution)/shard_map/all_gather | solution.py:23
  8.0 398.4 %all-reduce.2.cloned.1.call-start = ((), (), s32[]{:S(2)}) async-start(), calls=%async_computation.1 | async-start | bytes 4194304 | tf_op jit(solution)/shard_map/psum | solution.py:26
  52.0 193.3 %copy-start.2 = (s32[8]{0:T(128)S(1)}, s32[8]{0:T(128)}, u32[]{:S(2)}) copy-start(s32[8]{0:T(128)} %param.11) | copy-start | bytes 100
  52.0 452.7 %all-gather.6.cloned.1.call-start = ((), (), s32[]{:S(2)}) async-start(), calls=%async_computation | async-start | bytes 2228224 | tf_op jit(solution)/shard_map/all_gather | solution.py:27
  245.4 262.6 %copy-start.1 = (s32[1,1024]{1,0:T(1,128)S(1)}, s32[1,1024]{1,0:T(1,128)}, u32[]{:S(2)}) copy-start(s32[1,1024]{1,0:T(1,128)} %param.10) | copy-start | bytes 12292
Sparse Core Ops, SparseCore 0:
  9.5 37.5 all-gather.9
  49.1 190.9 all-gather.7
  243.1 163.2 all-reduce.1
  409.4 95.2 all-gather.5
where the time goes:
time: 534 us; the launch traced here: 529 us
  waiting for transfers between devices  488 us (91%)
  matrix products  13.5 us (3%)
  blocking collectives  13.4 us (3%)
  between operations  13.1 us (2%)
    all_gather x1, waiting for transfers between devices, on_device(): val_acts = lax.all_gather(val_act[0], ('dp', 'tensor'), axis=0, tiled=True)  188 us
    psum x1, waiting for transfers between devices, on_device(): grad_total = lax.psum(rows_gram(grad_rows, val_grads), 'tensor')  161 us
    all_gather x1, waiting for transfers between devices, on_device(): act_all = lax.all_gather(act_gram, 'tensor', axis=0, tiled=True)  98.4 us
    all_gather x1, waiting for transfers between devices, on_device(): val_grads = lax.all_gather(val_grad[0], 'dp', axis=0, tiled=True)  39 us
    psum x1, blocking collectives, on_device(): totals = lax.psum(local_terms, 'section')  13.4 us
  transfers between devices with their start and end apart: 4, of which 4 were waited for; matrix products, arithmetic and copies ran while one was open for 2% of the time, Pallas kernels for 0%

commit v1 on v0

v1 whole, which is shorter than its diff:
```python
import jax
import jax.numpy as jnp
from jax import lax
from jax.sharding import Mesh, PartitionSpec as P

SEQ_DEV = 4
VSEQ = 8
VLEN = 64
VLIVE = 384

NAMES = ("section", "pair", "core", "far", "depth")
SHAPE = (8, 2, 2, 2, 8)
PLANE = ("pair", "core", "far", "depth")
SLICES = ("pair", "core", "far")
TENSOR = ("far", "depth")
LAYERS = ("section", "far", "depth")


def swap(value, axis):
    return lax.ppermute(value, axis, [(0, 1), (1, 0)])


def trade(value, axes):
    return lax.all_to_all(value, axes, 0, 0, tiled=True)


def rows_gram(left, right):
    dims = (((1,), (1,)), ((), ()))
    return lax.dot_general(left, right, dims, preferred_element_type=jnp.float32)


def on_device(train_act, train_grad, val_act, val_grad, segment_ids, val_lengths):
    tok_count = segment_ids.shape[1]
    rows, width = train_act.shape[1:]
    val_rows = val_act.shape[1]
    parts = lax.axis_size(SLICES)
    planes = lax.axis_size(PLANE)
    depth = lax.axis_size("depth")
    sharers = lax.axis_size(TENSOR)
    piece = width // parts
    slots = VSEQ * VLEN

    positions = jnp.arange(VLEN, dtype=jnp.int32)
    starts = jnp.cumsum(val_lengths) - val_lengths
    rank = jnp.where(positions[None, :] < val_lengths[:, None], starts[:, None] + positions[None, :], -1)
    live_index = jnp.arange(VLIVE, dtype=jnp.int32)
    pick = (rank.reshape(1, slots) == live_index[:, None]).astype(jnp.bfloat16)

    own = val_grad[0]
    across = swap(own, "pair")
    beside = swap(own, "core")
    corner = swap(across, "core")

    acts = val_act[0].reshape(val_rows, parts, piece).transpose(1, 0, 2)
    acts = jnp.broadcast_to(acts[:, None], (parts, depth, val_rows, piece))
    val_acts = trade(acts.reshape(planes, val_rows, piece), PLANE).reshape(slots, piece)
    train_acts = trade(train_act[0].reshape(rows, parts, piece).transpose(1, 0, 2), SLICES)

    here = lax.axis_index("pair") * 2 + lax.axis_index("core")
    order = jnp.stack([here, here ^ 1, here ^ 2, here ^ 3])
    ranks = rank.reshape(4, slots // 4)[order].reshape(1, slots)
    pick_grad = (ranks == live_index[:, None]).astype(jnp.bfloat16)
    val_grads = jnp.concatenate([own, beside, across, corner], axis=0)
    live_grads = jnp.dot(pick_grad, val_grads, preferred_element_type=jnp.float32).astype(jnp.bfloat16)
    grad_part = rows_gram(train_grad[0], live_grads)
    grad_gram = jnp.sum(trade(grad_part.reshape(sharers, rows, VLIVE), TENSOR), axis=0)

    live_acts = jnp.dot(pick, val_acts, preferred_element_type=jnp.float32).astype(jnp.bfloat16)
    act_part = rows_gram(train_acts.reshape(parts * rows, piece), live_acts)
    act_gram = jnp.sum(trade(act_part.reshape(parts, rows, VLIVE), SLICES), axis=0)

    per_token = jnp.sum(act_gram * grad_gram, axis=1)
    first = lax.axis_index(TENSOR) * rows
    ids = lax.dynamic_slice(segment_ids[0], (first,), (rows,))
    seq_numbers = jnp.arange(SEQ_DEV, dtype=jnp.int32)[:, None]
    terms = jnp.sum(jnp.where(ids[None, :] == seq_numbers, per_token[None, :], 0.0), axis=1)
    everyone = lax.axis_size(LAYERS)
    totals = jnp.sum(trade(jnp.broadcast_to(terms, (everyone, 1, SEQ_DEV)), LAYERS), axis=0)
    norm_factor = jnp.sqrt(jnp.float32(tok_count * slots * lax.axis_size("section")))
    return totals / norm_factor


def solution(mesh):
    split = Mesh(mesh.devices.reshape(SHAPE), NAMES)
    placed = (
        P("section", PLANE, None),
        P("section", ("pair", "core"), TENSOR),
        P("section", PLANE, None),
        P("section", ("pair", "core"), TENSOR),
        P(("pair", "core"), None),
        P(),
    )
    return jax.shard_map(
        on_device, mesh=split, in_specs=placed, out_specs=P(("pair", "core"), None), check_vma=False
    )
```

time: 534 us -> 153 us (0.29)
  waiting for transfers between devices: 488 us -> 49.4 us
  blocking collectives: 13.4 us -> 48.2 us
  starting transfers between devices: 0.12 us -> 27.7 us
  between operations: 13.1 us -> 0.15 us
  local copies, waits for them, and re-layouts: 0.1 us -> 10.3 us
  other arithmetic: 0.59 us -> 8.19 us
  matrix products: 13.5 us -> 8.07 us
    all_gather x3 -> x0, waiting for transfers between devices: 325 us -> none  [the longest x1 188 us: on_device(): val_acts = lax.all_gather(val_act[0], ('dp', 'tensor'), axis=0, tiled=True)]
    psum x1 -> x0, waiting for transfers between devices: 161 us -> none  [on_device(): grad_total = lax.psum(rows_gram(grad_rows, val_grads), 'tensor')]
    all_to_all x0 -> x2, blocking collectives: none -> 48.2 us  [trade(): return lax.all_to_all(value, axes, 0, 0, tiled=True)]
    all_to_all x0 -> x3, waiting for transfers between devices: none -> 38.6 us  [trade(): return lax.all_to_all(value, axes, 0, 0, tiled=True)]
    all_to_all x0 -> x3, starting transfers between devices: none -> 18.8 us  [trade(): return lax.all_to_all(value, axes, 0, 0, tiled=True)]
    psum x1 -> x0, blocking collectives: 13.4 us -> none  [on_device(): totals = lax.psum(local_terms, 'section')]
    ppermute x0 -> x3, waiting for transfers between devices: none -> 10.9 us  [swap(): return lax.ppermute(value, axis, [(0, 1), (1, 0)])]
    ppermute x0 -> x3, starting transfers between devices: none -> 8.87 us  [swap(): return lax.ppermute(value, axis, [(0, 1), (1, 0)])]
  transfers between devices with their start and end apart: 4 -> 6, of which waited for: 4 -> 3; matrix products, arithmetic and copies ran while one was open for 2% -> 13% of each run, Pallas kernels for 0% -> 0%
where the time goes in v1:
time: 153 us; the launch traced here: 152 us
  waiting for transfers between devices  49.4 us (32%)
  blocking collectives  48.2 us (32%)
  starting transfers between devices  27.7 us (18%)
  local copies, waits for them, and re-layouts  10.3 us (7%)
  other arithmetic  8.19 us (5%)
  matrix products  8.07 us (5%)
    all_to_all x2, blocking collectives, trade(): return lax.all_to_all(value, axes, 0, 0, tiled=True)  48.2 us
    all_to_all x3, waiting for transfers between devices, trade(): return lax.all_to_all(value, axes, 0, 0, tiled=True)  38.6 us
    all_to_all x3, starting transfers between devices, trade(): return lax.all_to_all(value, axes, 0, 0, tiled=True)  18.8 us
    ppermute x3, waiting for transfers between devices, swap(): return lax.ppermute(value, axis, [(0, 1), (1, 0)])  10.9 us
    ppermute x3, starting transfers between devices, swap(): return lax.ppermute(value, axis, [(0, 1), (1, 0)])  8.87 us
    dot_general x2, matrix products, rows_gram(): lax.dot_general(left, right, dims, preferred_element_type=jnp.float32)  8.07 us
    dot_general x2, local copies, waits for them, and re-layouts, rows_gram(): lax.dot_general(left, right, dims, preferred_element_type=jnp.float32)  5.31 us
  transfers between devices with their start and end apart: 6, of which 3 were waited for; matrix products, arithmetic and copies ran while one was open for 13% of the time, Pallas kernels for 0%

profile of v1, /device:TPU:1, one launch (start us, length us, event | category | flops | bytes accessed | tf_op | source)
XLA Modules:
  0.0 152.0 jit_solution(1561364205428446008)
XLA Ops:
  0.0 0.0 copy-start
  0.0 0.0 copy-start.1
  0.0 1.3 copy.23
  1.3 0.0 copy-start.2
  1.3 0.1 copy.18
  1.4 20.8 %all_to_all.25 = bf16[8,64,640]{2,1,0:T(8,128)(2,1)} all-to-all(bf16[8,64,640]{2,1,0:T(8,128)(2,1)S(1)} %copy.18), channel_id=1, replica_groups=mesh['section'=8,'pair'=2,'core'=2,'far'=2,'depth'=8] {'pair','core','far'}, dimensions={0} | all-to-all | bytes 1310720 | tf_op jit(solution)/shard_map/all_to_all | solution.py:24
  22.3 0.0 copy-done.1
  22.3 0.9 broadcast_in_dim.19
  23.2 8.3 %all-to-all-start = ((bf16[64,8,640]{2,1,0:T(8,128)(2,1)}), bf16[64,8,640]{2,1,0:T(8,128)(2,1)}, u32[]{:S(2)}, u32[]{:S(2)}) async-start(bf16[64,8,640]{2,1,0:T(8,128)(2,1)} %bitcast.43), calls=%async_computation | async-start | bytes 1310720 | tf_op jit(solution)/shard_map/all_to_all | solution.py:24
  31.5 3.5 %collective-permute-start.1 = (bf16[128,1728]{0,1:T(8,128)(2,1)}, bf16[128,1728]{0,1:T(8,128)(2,1)}, u32[]{:S(2)}, u32[]{:S(2)}) collective-permute-start(bf16[128,1728]{0,1:T(8,128)(2,1)} %bitcast.50), channel_id=1, source_target_pairs={{0,32},{32,0},{1,33},{33,1},{2,34},{34,2},{3,35},{35,3},{4,36},{36... | collective-permute-start | bytes 1327112 | tf_op jit(solution)/shard_map/ppermute | solution.py:20
  34.9 2.5 %collective-permute-start = (bf16[128,1728]{0,1:T(8,128)(2,1)}, bf16[128,1728]{0,1:T(8,128)(2,1)}, u32[]{:S(2)}, u32[]{:S(2)}) collective-permute-start(bf16[128,1728]{0,1:T(8,128)(2,1)} %bitcast.51), channel_id=1, source_target_pairs={{0,16},{16,0},{1,17},{17,1},{2,18},{18,2},{3,19},{19,3},{4,20},{20... | collective-permute-start | bytes 1327112 | tf_op jit(solution)/shard_map/ppermute | solution.py:20
  37.4 0.0 copy-done.2
  37.4 0.1 lt.62
  37.5 0.2 reduce-window.9
  37.7 0.0 copy-start.3
  37.7 0.1 add.48
  37.8 0.1 add.49
  37.9 0.1 add.50
  37.9 0.3 copy-done.3
  38.2 0.1 lt.63
  38.3 0.1 lt.64
  38.4 0.6 lt.60
  38.9 0.7 add_select_fusion
  39.7 0.6 add_select_fusion.1
  40.2 10.9 %collective-permute-done.1 = bf16[128,1728]{0,1:T(8,128)(2,1)} collective-permute-done((bf16[128,1728]{0,1:T(8,128)(2,1)}, bf16[128,1728]{0,1:T(8,128)(2,1)}, u32[]{:S(2)}, u32[]{:S(2)}) %collective-permute-start.1) | collective-permute-done | bytes 442400 | tf_op jit(solution)/shard_map/ppermute | solution.py:20
  51.1 2.9 %collective-permute-start.2 = (bf16[128,1728]{0,1:T(8,128)(2,1)}, bf16[128,1728]{0,1:T(8,128)(2,1)}, u32[]{:S(2)}, u32[]{:S(2)}) collective-permute-start(bf16[128,1728]{0,1:T(8,128)(2,1)} %collective-permute-done.1), channel_id=1, source_target_pairs={{0,16},{16,0},{1,17},{17,1},{2,18},{18,2},{3,19},{19,3},{4,20},{20... | collective-permute-start | bytes 1327112 | tf_op jit(solution)/shard_map/ppermute | solution.py:20
  54.1 0.1 fusion.20
  54.2 0.1 select_n.33
  54.2 0.0 all-to-all-done
  54.2 3.0 %convolution_bitcast_fusion = f32[512,384]{0,1:T(8,128)} fusion(bf16[512,640]{1,0:T(8,128)(2,1)} %bitcast.46, bf16[64,8,640]{2,1,0:T(8,128)(2,1)} %all-to-all-done, s32[512]{0:T(512)S(1)} %select_n.33), kind=kOutput, calls=%fused_computation.12 | convolution fusion | flops 503758848 | bytes 2099200 | tf_op jit(solution)/shard_map/dot_general | solution.py:29
  57.2 2.3 %copy.19 = f32[512,384]{1,0:T(8,128)} copy(f32[512,384]{0,1:T(8,128)} %convolution_bitcast_fusion) | data formatting | bytes 1572864 | tf_op jit(solution)/shard_map/dot_general | solution.py:29
  59.5 4.4 %all-to-all-start.2 = ((f32[8,64,384]{2,1,0:T(8,128)}), f32[8,64,384]{2,1,0:T(8,128)}, u32[]{:S(2)}, u32[]{:S(2)}) async-start(f32[8,64,384]{2,1,0:T(8,128)} %bitcast.42), calls=%async_computation.2 | async-start | bytes 1572864 | tf_op jit(solution)/shard_map/all_to_all | solution.py:24
  63.9 0.6 gather_fusion
  64.4 0.0 collective-permute-done
  64.4 0.0 collective-permute-done.2
  64.4 0.0 copy-done
  64.5 5.1 %fusion.9 = f32[1024,384]{0,1:T(8,128)} fusion(bf16[1,1024,1728]{1,2,0:T(8,128)(2,1)S(1)} %copy-done, bf16[128,1728]{0,1:T(8,128)(2,1)} %collective-permute-done.2, bf16[128,1728]{0,1:T(8,128)(2,1)} %collective-permute-done.1, bf16[128,1728]{0,1:T(8,128)(2,1)} %collective-permute-done, bf16[128,1728]{0,1:T(8,128)(2,1)} %bitcast.52, s32[512]{0:T(512)S(1)} %bitcast.48), kind=kOutput, calls=%fused_computation.11 | convolution fusion | flops 2046369792 | bytes 6883328 | tf_op jit(solution)/shard_map/dot_general | solution.py:29
  69.6 3.0 %copy.20 = f32[1024,384]{1,0:T(8,128)} copy(f32[1024,384]{0,1:T(8,128)} %fusion.9) | data formatting | bytes 3145728 | tf_op jit(solution)/shard_map/dot_general | solution.py:29
  72.6 3.6 %all-to-all-done.2 = f32[8,64,384]{2,1,0:T(8,128)} async-done(((f32[8,64,384]{2,1,0:T(8,128)}), f32[8,64,384]{2,1,0:T(8,128)}, u32[]{:S(2)}, u32[]{:S(2)}) %all-to-all-start.2) | async-done | bytes 786464 | tf_op jit(solution)/shard_map/all_to_all | solution.py:24
  76.1 6.1 %all-to-all-start.3 = ((f32[16,64,384]{2,1,0:T(8,128)}), f32[16,64,384]{2,1,0:T(8,128)}, u32[]{:S(2)}, u32[]{:S(2)}) async-start(f32[16,64,384]{2,1,0:T(8,128)} %bitcast.41), calls=%async_computation.3 | async-start | bytes 3145728 | tf_op jit(solution)/shard_map/all_to_all | solution.py:24
  82.3 0.7 dynamic-slice_bitcast_fusion
  83.0 1.8 %reduce_sum.45 = f32[64,384]{1,0:T(8,128)} reduce(f32[8,64,384]{2,1,0:T(8,128)} %all-to-all-done.2, f32[]{:T(128)} %constant.37.clone.1), dimensions={0}, to_apply=%region_1.2 | reduce | flops 172032 | bytes 884740 | tf_op jit(solution)/shard_map/reduce_sum | solution.py:70
  84.8 35.0 %all-to-all-done.3 = f32[16,64,384]{2,1,0:T(8,128)} async-done(((f32[16,64,384]{2,1,0:T(8,128)}), f32[16,64,384]{2,1,0:T(8,128)}, u32[]{:S(2)}, u32[]{:S(2)}) %all-to-all-start.3) | async-done | bytes 1572896 | tf_op jit(solution)/shard_map/all_to_all | solution.py:24
  119.8 2.1 %reduce_sum.46 = f32[64,384]{1,0:T(8,128)} reduce(f32[16,64,384]{2,1,0:T(8,128)} %all-to-all-done.3, f32[]{:T(128)} %constant.37.clone.1), dimensions={0}, to_apply=%region_2.3 | reduce | flops 368640 | bytes 1671172 | tf_op jit(solution)/shard_map/reduce_sum | solution.py:66
  122.0 1.1 multiply_reduce_fusion
  123.0 0.1 select_reduce_fusion
  123.2 27.3 %all_to_all.26 = f32[128,1,4]{2,1,0:T(1,128)} all-to-all(f32[128,1,4]{2,1,0:T(1,128)S(1)} %broadcast_in_dim.42), channel_id=1, replica_groups=mesh['section'=8,'pair'=2,'core'=2,'far'=2,'depth'=8] {'section','far','..., dimensions={0} | all-to-all | bytes 4096 | tf_op jit(solution)/shard_map/all_to_all | solution.py:24
  150.5 1.0 reduce_sum.49
  151.5 0.5 multiply_bitcast_fusion
  (4 shorter events, 0.1 us)
Async XLA Ops:
  0.0 64.4 %copy-start = (bf16[1,1024,1728]{1,2,0:T(8,128)(2,1)S(1)}, bf16[1,1024,1728]{1,2,0:T(8,128)(2,1)}, u32[]{:S(2)}) copy-start(bf16[1,1024,1728]{1,2,0:T(8,128)(2,1)} %param.7) | copy-start | bytes 10616836
  0.0 22.3 %copy-start.1 = (bf16[1,8,5120]{2,1,0:T(8,128)(2,1)S(1)}, bf16[1,8,5120]{2,1,0:T(8,128)(2,1)}, u32[]{:S(2)}) copy-start(bf16[1,8,5120]{2,1,0:T(8,128)(2,1)} %param.8) | copy-start | bytes 245764
  1.3 36.1 %copy-start.2 = (s32[8]{0:T(128)S(1)}, s32[8]{0:T(128)}, u32[]{:S(2)}) copy-start(s32[8]{0:T(128)} %param.11) | copy-start | bytes 100
  23.2 31.1 %all-to-all-start = ((bf16[64,8,640]{2,1,0:T(8,128)(2,1)}), bf16[64,8,640]{2,1,0:T(8,128)(2,1)}, u32[]{:S(2)}, u32[]{:S(2)}) async-start(bf16[64,8,640]{2,1,0:T(8,128)(2,1)} %bitcast.43), calls=%async_computation | async-start | bytes 1310720 | tf_op jit(solution)/shard_map/all_to_all | solution.py:24
  31.5 19.7 %collective-permute-start.1 = (bf16[128,1728]{0,1:T(8,128)(2,1)}, bf16[128,1728]{0,1:T(8,128)(2,1)}, u32[]{:S(2)}, u32[]{:S(2)}) collective-permute-start(bf16[128,1728]{0,1:T(8,128)(2,1)} %bitcast.50), channel_id=1, source_target_pairs={{0,32},{32,0},{1,33},{33,1},{2,34},{34,2},{3,35},{35,3},{4,36},{36... | collective-permute-start | bytes 1327112 | tf_op jit(solution)/shard_map/ppermute | solution.py:20
  34.9 29.5 %collective-permute-start = (bf16[128,1728]{0,1:T(8,128)(2,1)}, bf16[128,1728]{0,1:T(8,128)(2,1)}, u32[]{:S(2)}, u32[]{:S(2)}) collective-permute-start(bf16[128,1728]{0,1:T(8,128)(2,1)} %bitcast.51), channel_id=1, source_target_pairs={{0,16},{16,0},{1,17},{17,1},{2,18},{18,2},{3,19},{19,3},{4,20},{20... | collective-permute-start | bytes 1327112 | tf_op jit(solution)/shard_map/ppermute | solution.py:20
  37.7 0.5 copy-start.3
  51.1 13.3 %collective-permute-start.2 = (bf16[128,1728]{0,1:T(8,128)(2,1)}, bf16[128,1728]{0,1:T(8,128)(2,1)}, u32[]{:S(2)}, u32[]{:S(2)}) collective-permute-start(bf16[128,1728]{0,1:T(8,128)(2,1)} %collective-permute-done.1), channel_id=1, source_target_pairs={{0,16},{16,0},{1,17},{17,1},{2,18},{18,2},{3,19},{19,3},{4,20},{20... | collective-permute-start | bytes 1327112 | tf_op jit(solution)/shard_map/ppermute | solution.py:20
  59.5 16.7 %all-to-all-start.2 = ((f32[8,64,384]{2,1,0:T(8,128)}), f32[8,64,384]{2,1,0:T(8,128)}, u32[]{:S(2)}, u32[]{:S(2)}) async-start(f32[8,64,384]{2,1,0:T(8,128)} %bitcast.42), calls=%async_computation.2 | async-start | bytes 1572864 | tf_op jit(solution)/shard_map/all_to_all | solution.py:24
  76.1 43.7 %all-to-all-start.3 = ((f32[16,64,384]{2,1,0:T(8,128)}), f32[16,64,384]{2,1,0:T(8,128)}, u32[]{:S(2)}, u32[]{:S(2)}) async-start(f32[16,64,384]{2,1,0:T(8,128)} %bitcast.41), calls=%async_computation.3 | async-start | bytes 3145728 | tf_op jit(solution)/shard_map/all_to_all | solution.py:24

commit v2 on v1

v2 whole, which is shorter than its diff:
```python
import functools
import jax
import jax.numpy as jnp
from jax import lax
from jax.experimental import pallas as pl
from jax.experimental.pallas import tpu as pltpu
from jax.sharding import Mesh, PartitionSpec as P

SEQ_DEV = 4
VSEQ = 8
VLEN = 64
SLOTS = VSEQ * VLEN
LIVE = 384
TILE = 512

NAMES = ("section", "pair", "core", "far", "depth")
SHAPE = (8, 2, 2, 2, 8)
PLANE = ("pair", "core", "far", "depth")
SLICES = ("core", "pair", "far")
ACROSS = ("core", "pair", "far", "depth")
TENSOR = ("far", "depth")
LAYERS = ("section", "far", "depth")

SMEM = pl.BlockSpec(memory_space=pltpu.SMEM)
VMEM = pl.BlockSpec(memory_space=pltpu.VMEM)
LIMIT = 48 * 1024 * 1024


def swap(value, axis):
    return lax.ppermute(value, axis, [(0, 1), (1, 0)])


def trade(value, axes):
    return lax.all_to_all(value, axes, 0, 0, tiled=True)


def dot(left, right, over):
    return lax.dot_general(left, right, (over, ((), ())), preferred_element_type=jnp.float32)


def params(**more):
    return pltpu.CompilerParams(vmem_limit_bytes=LIMIT, **more)


def cost(flops, moved):
    return pl.CostEstimate(flops=flops, bytes_accessed=moved, transcendentals=0)


def live_places(lens, seq, pos):
    place = jnp.full(seq.shape, -1, jnp.int32)
    start = jnp.int32(0)
    for number in range(VSEQ):
        count = lens[number]
        place = jnp.where((seq == number) & (pos < count), start + pos, place)
        start = start + count
    return place


def picker(place):
    wanted = lax.broadcasted_iota(jnp.int32, (LIVE, place.shape[1]), 0)
    return jnp.where(wanted == place, 1.0, 0.0).astype(jnp.bfloat16)


def live_part(spot, lens, pieces, first):
    here = spot[0] * 2 + spot[1]
    lane = lax.broadcasted_iota(jnp.int32, (1, SLOTS // 2), 1)
    quarter = SLOTS // 4
    owner = jnp.where(lane < quarter, here ^ first, here ^ (first + 1))
    within = lane % quarter
    place = live_places(lens, owner * 2 + within // VLEN, within % VLEN)
    both = jnp.concatenate([pieces[0][...], pieces[1][...]], axis=1)
    return dot(picker(place), both, ((1,), (1,))).astype(jnp.bfloat16)


def near_kernel(spot, lens, own, beside, near):
    near[...] = live_part(spot, lens, (own, beside), 0)


def near_call(spot, lens, own, beside):
    feats = own.shape[0]
    return pl.pallas_call(
        near_kernel,
        out_shape=jax.ShapeDtypeStruct((LIVE, feats), jnp.bfloat16),
        in_specs=[SMEM, SMEM, VMEM, VMEM],
        out_specs=VMEM,
        compiler_params=params(),
        cost_estimate=cost(SLOTS * LIVE * feats, SLOTS * feats + 2 * LIVE * feats),
    )(spot, lens, own, beside)


def grad_kernel(spot, lens, near, across, corner, train, out, live):
    @pl.when(pl.program_id(0) == 0)
    def _():
        live[...] = near[...] + live_part(spot, lens, (across, corner), 2)

    out[...] = dot(live[...], train[...], ((1,), (0,))).T.reshape(out.shape)


def grad_call(spot, lens, near, across, corner, train, rows):
    feats, toks = train.shape
    depth = toks // (2 * rows)
    step = TILE // rows
    half = depth // step
    quarter = pl.BlockSpec((feats, SLOTS // 4), lambda i, spot, lens: (0, 0))
    return pl.pallas_call(
        grad_kernel,
        out_shape=jax.ShapeDtypeStruct((depth, 2, rows, LIVE), jnp.float32),
        grid_spec=pltpu.PrefetchScalarGridSpec(
            num_scalar_prefetch=2,
            grid=(toks // TILE,),
            in_specs=[
                pl.BlockSpec((LIVE, feats), lambda i, spot, lens: (0, 0)),
                quarter,
                quarter,
                pl.BlockSpec((feats, TILE), lambda i, spot, lens: (0, i)),
            ],
            out_specs=pl.BlockSpec((step, 1, rows, LIVE), lambda i, spot, lens: (i % half, i // half, 0, 0)),
            scratch_shapes=[pltpu.VMEM((LIVE, feats), jnp.bfloat16)],
        ),
        compiler_params=params(),
        cost_estimate=cost(2 * toks * LIVE * feats, 2 * toks * feats + 4 * toks * LIVE),
    )(spot, lens, near, across, corner, train)


def act_kernel(lens, mine, came, vals, away, keep):
    slots = vals.shape[0]
    lane = lax.broadcasted_iota(jnp.int32, (1, slots), 1)
    block = lane // VLEN
    seq = (block // 2 % 2) * 4 + (block // 4) * 2 + block % 2
    chosen = picker(live_places(lens, seq, lane % VLEN))
    live = dot(chosen, vals[...], ((1,), (0,))).astype(jnp.bfloat16)
    for flip, ref in enumerate((keep, away)):
        left = jnp.concatenate([part[pair, flip] for part in (mine, came) for pair in range(2)], axis=0)
        ref[...] = dot(left, live, ((1,), (1,))).reshape(ref.shape)


def act_call(lens, mine, came, vals):
    rows, piece = mine.shape[2:]
    shape = jax.ShapeDtypeStruct((2, 2, rows, LIVE), jnp.float32)
    count = 8 * rows
    return pl.pallas_call(
        act_kernel,
        out_shape=(shape, shape),
        in_specs=[SMEM, VMEM, VMEM, VMEM],
        out_specs=(VMEM, VMEM),
        compiler_params=params(),
        cost_estimate=cost(2 * (count + SLOTS) * LIVE * piece, 4 * SLOTS * piece + 4 * count * LIVE),
    )(lens, mine, came, vals)


def combine_kernel(spot, ids, act_a, act_b, grads, out):
    depth, _, rows, _ = grads.shape
    per = 128 // rows
    lane = lax.broadcasted_iota(jnp.int32, (8, 128), 1)
    seqs = lax.broadcasted_iota(jnp.int32, (8, rows), 0)
    total = jnp.zeros((8, LIVE), jnp.float32)
    for far in range(2):
        number = far * depth + spot[3]
        lanes = ids[:, pl.ds(pl.multiple_of((number // per) * 128, 128), 128)]
        owner = lanes[:, :rows]
        for turn in range(1, per):
            owner = jnp.where(number % per == turn, lanes[:, turn * rows : (turn + 1) * rows], owner)
        grad = grads[0, far]
        for other in range(1, depth):
            grad = grad + grads[other, far]
        flip = spot[2] ^ far
        terms = (act_a[flip] + act_b[1 - flip]) * grad
        total = total + lax.dot_general(
            jnp.where(seqs == owner, 1.0, 0.0), terms, (((1,), (0,)), ((), ())),
            precision=lax.Precision.HIGHEST, preferred_element_type=jnp.float32,
        )
    column = jnp.sum(total, axis=1, keepdims=True)
    square = lax.broadcasted_iota(jnp.int32, (8, 128), 0) == lane
    out[...] = jnp.sum(jnp.where(square, column, 0.0), axis=0, keepdims=True)


def combine_call(spot, ids, act_a, act_b, grads):
    return pl.pallas_call(
        combine_kernel,
        out_shape=jax.ShapeDtypeStruct((1, 128), jnp.float32),
        in_specs=[SMEM, VMEM, VMEM, VMEM, VMEM],
        out_specs=VMEM,
        compiler_params=params(),
        cost_estimate=cost(2 * grads.size, 4 * grads.size),
    )(spot, ids, act_a, act_b, grads)


def total_kernel(scale, terms, out):
    out[...] = jnp.sum(terms[...], axis=0, keepdims=True)[:, :SEQ_DEV] * scale


def on_device(train_act, train_grad, val_act, val_grad, segment_ids, val_lengths):
    tok_count = segment_ids.shape[1]
    rows, width = train_act.shape[1:]
    val_rows = val_act.shape[1]
    parts = lax.axis_size(SLICES)
    depth = lax.axis_size("depth")
    piece = width // parts
    pair, core, far, deep = (lax.axis_index(name) for name in PLANE)
    spot = jnp.stack([pair, core, far, deep]).astype(jnp.int32)

    own = val_grad[0].T
    across = swap(own, "pair")
    beside = swap(own, "core")
    corner = swap(across, "core")

    acts = val_act[0].reshape(val_rows, parts, piece).transpose(1, 0, 2)
    acts = jnp.broadcast_to(acts[:, None], (parts, depth, val_rows, piece))
    vals = trade(acts.reshape(parts * depth, val_rows, piece), ACROSS).reshape(SLOTS, piece)

    def step(value, index):
        left, right = jnp.split(value, 2, axis=-1)
        return jnp.where(index == 0, left, right), jnp.where(index == 0, right, left)

    kept, sent = step(train_act[0], core)
    came = swap(sent, "core")
    own_late, came = lax.optimization_barrier((own, came))
    near = near_call(spot, val_lengths, own_late, beside)
    kept, sent = step(jnp.stack([kept, came]), pair)
    sent, across = lax.optimization_barrier((sent, across))
    came = swap(sent, "pair")

    grad_part = grad_call(spot, val_lengths, near, across, corner, train_grad[0].T, rows)
    grad_part, came = lax.optimization_barrier((grad_part, came))
    grads = trade(grad_part, "depth")

    mine, sent = step(jnp.stack([kept, came]), far)
    came = swap(sent, "far")

    act_away, act_keep = act_call(val_lengths, mine, came, vals)
    halves = act_keep + swap(act_away, "core")
    act_mine = halves[:, 0] + swap(halves[:, 1], "pair")
    act_came = swap(act_mine, "far")

    terms = combine_call(spot, segment_ids, act_mine, act_came, grads)
    everyone = lax.axis_size(LAYERS)
    terms = trade(jnp.broadcast_to(terms[None], (everyone, 1, 128)), LAYERS).reshape(everyone, 128)
    norm = (tok_count * SLOTS * lax.axis_size("section")) ** -0.5
    return pl.pallas_call(
        functools.partial(total_kernel, norm),
        out_shape=jax.ShapeDtypeStruct((1, SEQ_DEV), jnp.float32),
        in_specs=[VMEM],
        out_specs=VMEM,
        compiler_params=params(),
    )(terms)


def solution(mesh):
    split = Mesh(mesh.devices.reshape(SHAPE), NAMES)
    placed = (
        P("section", PLANE, None),
        P("section", ("pair", "core"), TENSOR),
        P("section", PLANE, None),
        P("section", ("pair", "core"), TENSOR),
        P(("pair", "core"), None),
        P(),
    )
    return jax.shard_map(
        on_device, mesh=split, in_specs=placed, out_specs=P(("pair", "core"), None), check_vma=False
    )
```

time: 153 us -> 115 us (0.75)
  waiting for transfers between devices: 49.4 us -> 25.4 us
  blocking collectives: 48.2 us -> 25.6 us
  starting transfers between devices: 27.7 us -> 48.4 us
  Pallas kernels: 0 us -> 9.77 us
  local copies, waits for them, and re-layouts: 10.3 us -> 1.93 us
  matrix products: 8.07 us -> 0 us
  other arithmetic: 8.19 us -> 2.25 us
    all_to_all x3 -> x2, waiting for transfers between devices: 38.6 us -> 3.06 us  [trade(): return lax.all_to_all(value, axes, 0, 0, tiled=True)]
    all_to_all x2 -> x1, blocking collectives: 48.2 us -> 25.6 us  [trade(): return lax.all_to_all(value, axes, 0, 0, tiled=True)]
    ppermute x3 -> x9, starting transfers between devices: 8.87 us -> 28.1 us  [swap(): return lax.ppermute(value, axis, [(0, 1), (1, 0)])]
    ppermute x3 -> x9, waiting for transfers between devices: 10.9 us -> 22.3 us  [swap(): return lax.ppermute(value, axis, [(0, 1), (1, 0)])]
    pallas_call x0 -> x5, Pallas kernels: none -> 9.77 us  [the longest x1 5.6 us: grad_call(): pl.pallas_call(grad_kernel, out_shape=jax.ShapeDtypeStruct((depth, 2, row...]
    dot_general x2 -> x0, matrix products: 8.07 us -> none  [rows_gram(): lax.dot_general(left, right, dims, preferred_element_type=jnp.float32)]
    reduce_sum x5 -> x0, other arithmetic: 6.08 us -> none  [the longest x1 2.11 us: on_device(): jnp.sum(trade(grad_part.reshape(sharers, rows, VLIVE), TENSOR), axis=0)]
    dot_general x2 -> x0, local copies, waits for them, and re-layouts: 5.31 us -> none  [rows_gram(): lax.dot_general(left, right, dims, preferred_element_type=jnp.float32)]
  transfers between devices with their start and end apart: 6 -> 11, of which waited for: 3 -> 6; matrix products, arithmetic and copies ran while one was open for 13% -> 4% of each run, Pallas kernels for 0% -> 7%
where the time goes in v2:
time: 115 us; the launch traced here: 114 us
  starting transfers between devices  48.4 us (42%)
  blocking collectives  25.6 us (22%)
  waiting for transfers between devices  25.4 us (22%)
  Pallas kernels  9.77 us (8%)
  other arithmetic  2.25 us (2%)
  local copies, waits for them, and re-layouts  1.93 us (2%)
    ppermute x9, starting transfers between devices, swap(): return lax.ppermute(value, axis, [(0, 1), (1, 0)])  28.1 us
    all_to_all x1, blocking collectives, trade(): return lax.all_to_all(value, axes, 0, 0, tiled=True)  25.6 us
    ppermute x9, waiting for transfers between devices, swap(): return lax.ppermute(value, axis, [(0, 1), (1, 0)])  22.3 us
    all_to_all x2, starting transfers between devices, trade(): return lax.all_to_all(value, axes, 0, 0, tiled=True)  20.4 us
    pallas_call x1, Pallas kernels, grad_call(): pl.pallas_call(grad_kernel, out_shape=jax.ShapeDtypeStruct((depth, 2, row...  5.6 us
    all_to_all x2, waiting for transfers between devices, trade(): return lax.all_to_all(value, axes, 0, 0, tiled=True)  3.06 us
  transfers between devices with their start and end apart: 11, of which 6 were waited for; matrix products, arithmetic and copies ran while one was open for 4% of the time, Pallas kernels for 7%

profile of v2, /device:TPU:1, one launch (start us, length us, event | category | flops | bytes accessed | tf_op | source)
XLA Modules:
  0.0 113.6 jit_solution(10338399843582304331)
XLA Ops:
  0.0 0.0 copy-start.3
  0.0 4.1 %collective-permute-start.2 = (bf16[1728,128]{1,0:T(8,128)(2,1)}, bf16[1728,128]{1,0:T(8,128)(2,1)S(1)}, u32[]{:S(2)}, u32[]{:S(2)}) collective-permute-start(bf16[1728,128]{1,0:T(8,128)(2,1)} %bitcast.31), channel_id=1, source_target_pairs={{0,32},{32,0},{1,33},{33,1},{2,34},{34,2},{3,35},{35,3},{4,36},{36... | collective-permute-start | bytes 1327112 | tf_op jit(solution)/shard_map/ppermute | solution.py:30
  4.1 0.0 copy-start
  4.1 1.8 %broadcast_in_dim.6 = bf16[8,8,8,640]{3,2,1,0:T(8,128)(2,1)} broadcast(bf16[8,8,640]{2,1,0:T(8,128)(2,1)} %bitcast.39), dimensions={0,2,3} | broadcast | bytes 737280 | tf_op jit(solution)/shard_map/broadcast_in_dim | solution.py:208
  5.9 14.1 %all-to-all-start = ((bf16[64,8,640]{2,1,0:T(8,128)(2,1)}), bf16[64,8,640]{2,1,0:T(8,128)(2,1)S(1)}, u32[]{:S(2)}, u32[]{:S(2)}) async-start(bf16[64,8,640]{2,1,0:T(8,128)(2,1)} %bitcast.16), calls=%async_computation | async-start | bytes 1310720 | tf_op jit(solution)/shard_map/all_to_all | solution.py:34
  20.0 0.0 copy-start.2
  20.0 0.0 copy-done.3
  20.1 2.3 %collective-permute-start = (bf16[64,2560]{1,0:T(8,128)(2,1)S(1)}, bf16[64,2560]{1,0:T(8,128)(2,1)}, u32[]{:S(2)}, u32[]{:S(2)}) collective-permute-start(bf16[64,2560]{1,0:T(8,128)(2,1)S(1)} %get-tuple-element.26), channel_id=1, source_target_pairs={{0,16},{16,0},{1,17},{17,1},{2,18},{18,2},{3,19},{19,3},{4,20},{20... | collective-permute-start | bytes 983048 | tf_op jit(solution)/shard_map/ppermute | solution.py:30
  22.4 0.0 copy-done
  22.4 2.1 %collective-permute-start.1 = (bf16[1728,128]{1,0:T(8,128)(2,1)S(1)}, bf16[1728,128]{1,0:T(8,128)(2,1)S(1)}, u32[]{:S(2)}, u32[]{:S(2)}) collective-permute-start(bf16[1728,128]{1,0:T(8,128)(2,1)S(1)} %bitcast.32), channel_id=1, source_target_pairs={{0,16},{16,0},{1,17},{17,1},{2,18},{18,2},{3,19},{19,3},{4,20},{20... | collective-permute-start | bytes 1327112 | tf_op jit(solution)/shard_map/ppermute | solution.py:30
  24.4 0.0 collective-permute-done.2.across
  24.5 2.3 %collective-permute-start.3 = (bf16[1728,128]{1,0:T(8,128)(2,1)S(1)}, bf16[1728,128]{1,0:T(8,128)(2,1)S(1)}, u32[]{:S(2)}, u32[]{:S(2)}) collective-permute-start(bf16[1728,128]{1,0:T(8,128)(2,1)S(1)} %collective-permute-done.2.across), channel_id=1, source_target_pairs={{0,16},{16,0},{1,17},{17,1},{2,18},{18,2},{3,19},{19,3},{4,20},{20... | collective-permute-start | bytes 1327112 | tf_op jit(solution)/shard_map/ppermute | solution.py:30
  26.7 0.0 collective-permute-done
  26.7 1.9 %select_bitcast_fusion = (bf16[1,2,64,1280]{3,2,1,0:T(8,128)(2,1)S(1)}, bf16[2,64,1280]{2,1,0:T(8,128)(2,1)}) fusion(pred[]{:T(512)S(6)} %eq.13, bf16[1,64,2560]{2,1,0:T(8,128)(2,1)} %bitcast.8, bf16[1,64,2560]{2,1,0:T(8,128)(2,1)S(1)} %get-tuple-element.25), kind=kLoop, calls=%fused_computation.9 | loop fusion | flops 2293760 | bytes 1310721 | tf_op jit(solution)/shard_map/stack | solution.py:227
  28.7 3.2 %collective-permute-start.4 = (bf16[2,64,1280]{2,1,0:T(8,128)(2,1)}, bf16[2,64,1280]{2,1,0:T(8,128)(2,1)S(1)}, u32[]{:S(2)}, u32[]{:S(2)}) collective-permute-start(bf16[2,64,1280]{2,1,0:T(8,128)(2,1)} %get-tuple-element.16), channel_id=1, source_target_pairs={{0,32},{32,0},{1,33},{33,1},{2,34},{34,2},{3,35},{35,3},{4,36},{36... | collective-permute-start | bytes 983048 | tf_op jit(solution)/shard_map/ppermute | solution.py:30
  31.9 0.1 pad_add_fusion.spot
  32.0 0.0 collective-permute-done.1.beside
  32.0 0.0 copy-done.2
  32.0 1.1 shard_map.64.near
  33.1 0.0 collective-permute-done.3.corner
  33.1 5.6 %shard_map.65 = f32[8,2,64,384]{3,2,1,0:T(8,128)} custom-call(s32[4]{0:T(128)S(1)} %pad_add_fusion.spot, s32[8]{0:T(128)S(1)} %copy-done.2, bf16[384,1728]{1,0:T(8,128)(2,1)S(1)} %shard_map.64.near, bf16[1728,128]{1,0:T(8,128)(2,1)S(1)} %collective-permute-done.2.across, bf16[1728,128]{1,0:T(8,128)(2,1)S(1)} %collective-permute-done.3.corner, ...), custom_call_target="tpu_custom_call" | custom-call | flops 1358954496 | bytes 5111808 | tf_op jit(solution)/shard_map/pallas_call | solution.py:105
  38.7 3.2 %collective-permute-done.4 = bf16[2,64,1280]{2,1,0:T(8,128)(2,1)S(1)} collective-permute-done((bf16[2,64,1280]{2,1,0:T(8,128)(2,1)}, bf16[2,64,1280]{2,1,0:T(8,128)(2,1)S(1)}, u32[]{:S(2)}, u32[]{:S(2)}) %collective-permute-start.4) | collective-permute-done | bytes 327712 | tf_op jit(solution)/shard_map/ppermute | solution.py:30
  41.9 0.0 all-to-all-done
  41.9 6.3 %all-to-all-start.1 = ((f32[8,2,64,384]{3,2,1,0:T(8,128)}), f32[8,2,64,384]{3,2,1,0:T(8,128)S(1)}, u32[]{:S(2)}, u32[]{:S(2)}) async-start(f32[8,2,64,384]{3,2,1,0:T(8,128)} %shard_map.65), calls=%async_computation.1 | async-start | bytes 3145728 | tf_op jit(solution)/shard_map/all_to_all | solution.py:34
  48.2 0.1 broadcast_select_fusion.2
  48.3 3.8 %collective-permute-start.5 = (bf16[2,2,64,640]{3,2,1,0:T(8,128)(2,1)S(1)}, bf16[2,2,64,640]{3,2,1,0:T(8,128)(2,1)S(1)}, u32[]{:S(2)}, u32[]{:S(2)}) collective-permute-start(bf16[2,2,64,640]{3,2,1,0:T(8,128)(2,1)S(1)} %get-tuple-element.21), channel_id=1, source_target_pairs={{0,8},{8,0},{1,9},{9,1},{2,10},{10,2},{3,11},{11,3},{4,12},{12,4},... | collective-permute-start | bytes 983048 | tf_op jit(solution)/shard_map/ppermute | solution.py:30
  52.1 7.7 %collective-permute-done.5.came = bf16[2,2,64,640]{3,2,1,0:T(8,128)(2,1)S(1)} collective-permute-done((bf16[2,2,64,640]{3,2,1,0:T(8,128)(2,1)S(1)}, bf16[2,2,64,640]{3,2,1,0:T(8,128)(2,1)S(1)}, u32[]{:S(2)}, u32[]{:S(2)}) %collective-permute-start.5) | collective-permute-done | bytes 327712 | tf_op jit(solution)/shard_map/ppermute | solution.py:30
  59.8 1.6 %shard_map.66 = (f32[2,2,64,384]{3,2,1,0:T(8,128)S(1)}, f32[2,2,64,384]{3,2,1,0:T(8,128)S(1)}) custom-call(s32[8]{0:T(128)S(1)} %copy-done.2, bf16[2,2,64,640]{3,2,1,0:T(8,128)(2,1)S(1)} %get-tuple-element.22.mine, bf16[2,2,64,640]{3,2,1,0:T(8,128)(2,1)S(1)} %collective-permute-done.5.came, bf16[512,640]{1,0:T(8,128)(2,1)S(1)} %bitcast.30), custom_call_target="tpu_custom_call" | custom-call | flops 503316480 | bytes 2097152 | tf_op jit(solution)/shard_map/pallas_call | solution.py:141
  61.4 0.0 copy-start.1
  61.5 3.9 %collective-permute-start.6 = (f32[2,2,64,384]{3,2,0,1:T(8,128)S(1)}, f32[2,2,64,384]{3,2,0,1:T(8,128)S(1)}, u32[]{:S(2)}, u32[]{:S(2)}) collective-permute-start(f32[2,2,64,384]{3,2,0,1:T(8,128)S(1)} %copy.9), channel_id=1, source_target_pairs={{0,16},{16,0},{1,17},{17,1},{2,18},{18,2},{3,19},{19,3},{4,20},{20... | collective-permute-start | bytes 1179656 | tf_op jit(solution)/shard_map/ppermute | solution.py:30
  65.4 1.3 %collective-permute-done.6 = f32[2,2,64,384]{3,2,0,1:T(8,128)S(1)} collective-permute-done((f32[2,2,64,384]{3,2,0,1:T(8,128)S(1)}, f32[2,2,64,384]{3,2,0,1:T(8,128)S(1)}, u32[]{:S(2)}, u32[]{:S(2)}) %collective-permute-start.6) | collective-permute-done | bytes 393248 | tf_op jit(solution)/shard_map/ppermute | solution.py:30
  66.8 2.8 %collective-permute-start.7 = (f32[2,64,384]{2,1,0:T(8,128)S(1)}, f32[2,64,384]{2,1,0:T(8,128)S(1)}, u32[]{:S(2)}, u32[]{:S(2)}) collective-permute-start(f32[2,64,384]{2,1,0:T(8,128)S(1)} %slice_bitcast_fusion), channel_id=1, source_target_pairs={{0,32},{32,0},{1,33},{33,1},{2,34},{34,2},{3,35},{35,3},{4,36},{36... | collective-permute-start | bytes 589832 | tf_op jit(solution)/shard_map/ppermute | solution.py:30
  69.5 5.2 %collective-permute-done.7 = f32[2,64,384]{2,1,0:T(8,128)S(1)} collective-permute-done((f32[2,64,384]{2,1,0:T(8,128)S(1)}, f32[2,64,384]{2,1,0:T(8,128)S(1)}, u32[]{:S(2)}, u32[]{:S(2)}) %collective-permute-start.7) | collective-permute-done | bytes 196640 | tf_op jit(solution)/shard_map/ppermute | solution.py:30
  74.8 3.8 %collective-permute-start.8 = (f32[2,64,384]{2,1,0:T(8,128)S(1)}, f32[2,64,384]{2,1,0:T(8,128)S(1)}, u32[]{:S(2)}, u32[]{:S(2)}) collective-permute-start(f32[2,64,384]{2,1,0:T(8,128)S(1)} %fusion.2.act_a), channel_id=1, source_target_pairs={{0,8},{8,0},{1,9},{9,1},{2,10},{10,2},{3,11},{11,3},{4,12},{12,4},... | collective-permute-start | bytes 589832 | tf_op jit(solution)/shard_map/ppermute | solution.py:30
  78.6 4.8 %collective-permute-done.8.act_b = f32[2,64,384]{2,1,0:T(8,128)S(1)} collective-permute-done((f32[2,64,384]{2,1,0:T(8,128)S(1)}, f32[2,64,384]{2,1,0:T(8,128)S(1)}, u32[]{:S(2)}, u32[]{:S(2)}) %collective-permute-start.8) | collective-permute-done | bytes 196640 | tf_op jit(solution)/shard_map/ppermute | solution.py:30
  83.4 3.1 %all-to-all-done.1.grads = f32[8,2,64,384]{3,2,1,0:T(8,128)S(1)} async-done(((f32[8,2,64,384]{3,2,1,0:T(8,128)}), f32[8,2,64,384]{3,2,1,0:T(8,128)S(1)}, u32[]{:S(2)}, u32[]{:S(2)}) %all-to-all-start.1) | async-done | bytes 1572896 | tf_op jit(solution)/shard_map/all_to_all | solution.py:34
  86.4 0.0 copy-done.1
  86.4 1.0 shard_map.67
  87.4 0.1 broadcast_in_dim.16
  87.5 25.6 %all_to_all.15 = f32[128,1,128]{2,1,0:T(1,128)S(1)} all-to-all(f32[128,1,128]{2,1,0:T(1,128)S(1)} %broadcast_in_dim.16), channel_id=1, replica_groups=mesh['section'=8,'pair'=2,'core'=2,'far'=2,'depth'=8] {'section','far','..., dimensions={0} | all-to-all | bytes 131072 | tf_op jit(solution)/shard_map/all_to_all | solution.py:34
  113.1 0.5 shard_map.68
  (5 shorter events, 0.2 us)
Async XLA Ops:
  0.0 20.0 %copy-start.3 = (bf16[1,64,5120]{2,1,0:T(8,128)(2,1)S(1)}, bf16[1,64,5120]{2,1,0:T(8,128)(2,1)}, u32[]{:S(2)}) copy-start(bf16[1,64,5120]{2,1,0:T(8,128)(2,1)} %param.6) | copy-start | bytes 1966084
  0.0 24.4 %collective-permute-start.2 = (bf16[1728,128]{1,0:T(8,128)(2,1)}, bf16[1728,128]{1,0:T(8,128)(2,1)S(1)}, u32[]{:S(2)}, u32[]{:S(2)}) collective-permute-start(bf16[1728,128]{1,0:T(8,128)(2,1)} %bitcast.31), channel_id=1, source_target_pairs={{0,32},{32,0},{1,33},{33,1},{2,34},{34,2},{3,35},{35,3},{4,36},{36... | collective-permute-start | bytes 1327112 | tf_op jit(solution)/shard_map/ppermute | solution.py:30
  4.1 18.3 %copy-start = (bf16[1,128,1728]{1,2,0:T(8,128)(2,1)S(1)}, bf16[1,128,1728]{1,2,0:T(8,128)(2,1)}, u32[]{:S(2)}) copy-start(bf16[1,128,1728]{1,2,0:T(8,128)(2,1)} %param.9) | copy-start | bytes 1327108
  5.9 36.0 %all-to-all-start = ((bf16[64,8,640]{2,1,0:T(8,128)(2,1)}), bf16[64,8,640]{2,1,0:T(8,128)(2,1)S(1)}, u32[]{:S(2)}, u32[]{:S(2)}) async-start(bf16[64,8,640]{2,1,0:T(8,128)(2,1)} %bitcast.16), calls=%async_computation | async-start | bytes 1310720 | tf_op jit(solution)/shard_map/all_to_all | solution.py:34
  20.0 12.0 %copy-start.2 = (s32[8]{0:T(128)S(1)}, s32[8]{0:T(128)}, u32[]{:S(2)}) copy-start(s32[8]{0:T(128)} %lens.5) | copy-start | bytes 100
  20.1 6.6 %collective-permute-start = (bf16[64,2560]{1,0:T(8,128)(2,1)S(1)}, bf16[64,2560]{1,0:T(8,128)(2,1)}, u32[]{:S(2)}, u32[]{:S(2)}) collective-permute-start(bf16[64,2560]{1,0:T(8,128)(2,1)S(1)} %get-tuple-element.26), channel_id=1, source_target_pairs={{0,16},{16,0},{1,17},{17,1},{2,18},{18,2},{3,19},{19,3},{4,20},{20... | collective-permute-start | bytes 983048 | tf_op jit(solution)/shard_map/ppermute | solution.py:30
  22.4 9.6 %collective-permute-start.1 = (bf16[1728,128]{1,0:T(8,128)(2,1)S(1)}, bf16[1728,128]{1,0:T(8,128)(2,1)S(1)}, u32[]{:S(2)}, u32[]{:S(2)}) collective-permute-start(bf16[1728,128]{1,0:T(8,128)(2,1)S(1)} %bitcast.32), channel_id=1, source_target_pairs={{0,16},{16,0},{1,17},{17,1},{2,18},{18,2},{3,19},{19,3},{4,20},{20... | collective-permute-start | bytes 1327112 | tf_op jit(solution)/shard_map/ppermute | solution.py:30
  24.5 8.6 %collective-permute-start.3 = (bf16[1728,128]{1,0:T(8,128)(2,1)S(1)}, bf16[1728,128]{1,0:T(8,128)(2,1)S(1)}, u32[]{:S(2)}, u32[]{:S(2)}) collective-permute-start(bf16[1728,128]{1,0:T(8,128)(2,1)S(1)} %collective-permute-done.2.across), channel_id=1, source_target_pairs={{0,16},{16,0},{1,17},{17,1},{2,18},{18,2},{3,19},{19,3},{4,20},{20... | collective-permute-start | bytes 1327112 | tf_op jit(solution)/shard_map/ppermute | solution.py:30
  28.7 13.2 %collective-permute-start.4 = (bf16[2,64,1280]{2,1,0:T(8,128)(2,1)}, bf16[2,64,1280]{2,1,0:T(8,128)(2,1)S(1)}, u32[]{:S(2)}, u32[]{:S(2)}) collective-permute-start(bf16[2,64,1280]{2,1,0:T(8,128)(2,1)} %get-tuple-element.16), channel_id=1, source_target_pairs={{0,32},{32,0},{1,33},{33,1},{2,34},{34,2},{3,35},{35,3},{4,36},{36... | collective-permute-start | bytes 983048 | tf_op jit(solution)/shard_map/ppermute | solution.py:30
  41.9 44.5 %all-to-all-start.1 = ((f32[8,2,64,384]{3,2,1,0:T(8,128)}), f32[8,2,64,384]{3,2,1,0:T(8,128)S(1)}, u32[]{:S(2)}, u32[]{:S(2)}) async-start(f32[8,2,64,384]{3,2,1,0:T(8,128)} %shard_map.65), calls=%async_computation.1 | async-start | bytes 3145728 | tf_op jit(solution)/shard_map/all_to_all | solution.py:34
  48.3 11.5 %collective-permute-start.5 = (bf16[2,2,64,640]{3,2,1,0:T(8,128)(2,1)S(1)}, bf16[2,2,64,640]{3,2,1,0:T(8,128)(2,1)S(1)}, u32[]{:S(2)}, u32[]{:S(2)}) collective-permute-start(bf16[2,2,64,640]{3,2,1,0:T(8,128)(2,1)S(1)} %get-tuple-element.21), channel_id=1, source_target_pairs={{0,8},{8,0},{1,9},{9,1},{2,10},{10,2},{3,11},{11,3},{4,12},{12,4},... | collective-permute-start | bytes 983048 | tf_op jit(solution)/shard_map/ppermute | solution.py:30
  61.4 25.0 %copy-start.1 = (s32[1,1024]{1,0:T(1,128)S(1)}, s32[1,1024]{1,0:T(1,128)}, u32[]{:S(2)}) copy-start(s32[1,1024]{1,0:T(1,128)} %ids.1) | copy-start | bytes 12292
  61.5 5.2 %collective-permute-start.6 = (f32[2,2,64,384]{3,2,0,1:T(8,128)S(1)}, f32[2,2,64,384]{3,2,0,1:T(8,128)S(1)}, u32[]{:S(2)}, u32[]{:S(2)}) collective-permute-start(f32[2,2,64,384]{3,2,0,1:T(8,128)S(1)} %copy.9), channel_id=1, source_target_pairs={{0,16},{16,0},{1,17},{17,1},{2,18},{18,2},{3,19},{19,3},{4,20},{20... | collective-permute-start | bytes 1179656 | tf_op jit(solution)/shard_map/ppermute | solution.py:30
  66.8 8.0 %collective-permute-start.7 = (f32[2,64,384]{2,1,0:T(8,128)S(1)}, f32[2,64,384]{2,1,0:T(8,128)S(1)}, u32[]{:S(2)}, u32[]{:S(2)}) collective-permute-start(f32[2,64,384]{2,1,0:T(8,128)S(1)} %slice_bitcast_fusion), channel_id=1, source_target_pairs={{0,32},{32,0},{1,33},{33,1},{2,34},{34,2},{3,35},{35,3},{4,36},{36... | collective-permute-start | bytes 589832 | tf_op jit(solution)/shard_map/ppermute | solution.py:30
  74.8 8.6 %collective-permute-start.8 = (f32[2,64,384]{2,1,0:T(8,128)S(1)}, f32[2,64,384]{2,1,0:T(8,128)S(1)}, u32[]{:S(2)}, u32[]{:S(2)}) collective-permute-start(f32[2,64,384]{2,1,0:T(8,128)S(1)} %fusion.2.act_a), channel_id=1, source_target_pairs={{0,8},{8,0},{1,9},{9,1},{2,10},{10,2},{3,11},{11,3},{4,12},{12,4},... | collective-permute-start | bytes 589832 | tf_op jit(solution)/shard_map/ppermute | solution.py:30

commit v3 on v2

v3 whole, which is shorter than its diff:
```python
import functools
import jax
import jax.numpy as jnp
from jax import lax
from jax.experimental import pallas as pl
from jax.experimental.pallas import tpu as pltpu
from jax.sharding import Mesh, PartitionSpec as P

SEQ_DEV = 4
VSEQ = 8
VLEN = 64
SLOTS = VSEQ * VLEN
LIVE = 384
CODES = 32767.0

NAMES = ("section", "pair", "core", "far", "depth")
SHAPE = (8, 2, 2, 2, 8)
PLANE = ("pair", "core", "far", "depth")
SLICES = ("core", "pair", "far")
ACROSS = ("core", "pair", "far", "depth")
TENSOR = ("far", "depth")
LAYERS = ("section", "far", "depth")

SMEM = pl.BlockSpec(memory_space=pltpu.SMEM)
VMEM = pl.BlockSpec(memory_space=pltpu.VMEM)
LIMIT = 48 * 1024 * 1024


def swap(value, axis):
    return lax.ppermute(value, axis, [(0, 1), (1, 0)])


def swap_both(value):
    return lax.ppermute(value, ("pair", "far"), [(0, 3), (1, 2), (2, 1), (3, 0)])


def trade(value, axes):
    return lax.all_to_all(value, axes, 0, 0, tiled=True)


def dot(left, right, over):
    return lax.dot_general(left, right, (over, ((), ())), preferred_element_type=jnp.float32)


def params(**more):
    return pltpu.CompilerParams(vmem_limit_bytes=LIMIT, **more)


def cost(flops, moved):
    return pl.CostEstimate(flops=flops, bytes_accessed=moved, transcendentals=0)


def live_places(lens, seq, pos):
    place = jnp.full(seq.shape, -1, jnp.int32)
    start = jnp.int32(0)
    for number in range(VSEQ):
        count = lens[number]
        place = jnp.where((seq == number) & (pos < count), start + pos, place)
        start = start + count
    return place


def picker(place):
    wanted = lax.broadcasted_iota(jnp.int32, (LIVE, place.shape[1]), 0)
    return jnp.where(wanted == place, 1.0, 0.0).astype(jnp.bfloat16)


def spread_kernel(val, spread):
    count, _, piece = spread.shape
    parts = val.shape[1] // piece
    for part in range(parts):
        rows_here = val[:, part * piece : (part + 1) * piece]
        for turn in range(count // parts):
            spread[part * (count // parts) + turn] = rows_here


def spread_call(val, piece, count):
    return pl.pallas_call(
        spread_kernel,
        out_shape=jax.ShapeDtypeStruct((count, val.shape[0], piece), val.dtype),
        in_specs=[VMEM],
        out_specs=VMEM,
        compiler_params=params(),
        cost_estimate=cost(0, 2 * count * val.shape[0] * piece),
    )(val)


def beside_kernel(spot, own, train, beside):
    feats, rows = own.shape[0], train.shape[0]
    half = train.shape[1] // 2
    beside[0:feats, :] = own[...]
    for tile in range(half // 128):
        lanes = pl.ds(pl.multiple_of((1 - spot[1]) * half + tile * 128, 128), 128)
        beside[feats + tile * rows : feats + (tile + 1) * rows, :] = train[:, lanes]


def beside_call(spot, own, train):
    feats, lanes = own.shape
    extra = train.shape[0] * train.shape[1] // 2 // lanes
    return pl.pallas_call(
        beside_kernel,
        out_shape=jax.ShapeDtypeStruct((feats + extra, lanes), own.dtype),
        in_specs=[SMEM, VMEM, VMEM],
        out_specs=VMEM,
        compiler_params=params(),
        cost_estimate=cost(0, 4 * (own.size + train.size)),
    )(spot, own, train)


def slices_kernel(spot, train, got, own, to_pair, to_far, to_both):
    rows, piece = own.shape[1:]
    first = got.shape[0] - rows * (train.shape[1] // 2 // 128)
    per = piece // 128
    for flip, ref in enumerate((own, to_far, to_pair, to_both)):
        number = (spot[0] * 2 + spot[2]) ^ flip
        lanes = spot[1] * (train.shape[1] // 2) + number * piece
        ref[0] = train[:, pl.ds(pl.multiple_of(lanes, 128), piece)]
        for tile in range(per):
            at = pl.multiple_of(first + (number * per + tile) * rows, rows)
            ref[1, :, tile * 128 : (tile + 1) * 128] = got[pl.ds(at, rows), :]


def slices_call(spot, train, got, piece):
    shape = jax.ShapeDtypeStruct((2, train.shape[0], piece), train.dtype)
    return pl.pallas_call(
        slices_kernel,
        out_shape=(shape,) * 4,
        in_specs=[SMEM, VMEM, VMEM],
        out_specs=(VMEM,) * 4,
        compiler_params=params(),
        cost_estimate=cost(0, 8 * train.size),
    )(spot, train, got)


def live_part(spot, lens, left, right, first):
    here = spot[0] * 2 + spot[1]
    lane = lax.broadcasted_iota(jnp.int32, (1, SLOTS // 2), 1)
    quarter = SLOTS // 4
    owner = jnp.where(lane < quarter, here ^ first, here ^ (first + 1))
    within = lane % quarter
    place = live_places(lens, owner * 2 + within // VLEN, within % VLEN)
    return dot(picker(place), jnp.concatenate([left, right], axis=1), ((1,), (1,)))


def grad_kernel(spot, lens, own, beside, across, corner, train, out, scale):
    feats, toks = train.shape
    depth, _, rows, _ = out.shape
    near = live_part(spot, lens, own[...], beside[0:feats, :], 0)
    live = (near + live_part(spot, lens, across[...], corner[...], 2)).astype(jnp.bfloat16)
    for far in range(2):
        block = train[:, far * (toks // 2) : (far + 1) * (toks // 2)]
        gram = dot(live, block, ((1,), (0,))).T
        size = jnp.abs(gram)
        most = jnp.max(size)
        share = jnp.sqrt(size * jnp.where(most > 0.0, 1.0 / most, 0.0))
        code = jnp.round(jnp.where(gram < 0.0, -CODES, CODES) * share)
        out[:, far] = code.astype(jnp.int32).astype(jnp.int16).reshape(depth, rows, LIVE)
        scale[far * 8 : (far + 1) * 8, :] = jnp.full((8, 128), most, jnp.float32)


def grad_call(spot, lens, pieces, train, rows):
    feats, toks = train.shape
    return pl.pallas_call(
        grad_kernel,
        out_shape=(
            jax.ShapeDtypeStruct((toks // (2 * rows), 2, rows, LIVE), jnp.int16),
            jax.ShapeDtypeStruct((16, 128), jnp.float32),
        ),
        in_specs=[SMEM, SMEM] + [VMEM] * 5,
        out_specs=(VMEM, VMEM),
        compiler_params=params(),
        cost_estimate=cost(2 * toks * LIVE * feats, 2 * toks * feats + 4 * toks * LIVE),
    )(spot, lens, *pieces, train)


def act_kernel(lens, own, pair, far, both, vals, away, keep):
    slots = vals.shape[0]
    lane = lax.broadcasted_iota(jnp.int32, (1, slots), 1)
    block = lane // VLEN
    seq = (block // 2 % 2) * 4 + (block // 4) * 2 + block % 2
    chosen = picker(live_places(lens, seq, lane % VLEN))
    live = dot(chosen, vals[...], ((1,), (0,))).astype(jnp.bfloat16)
    for flip, ref in enumerate((keep, away)):
        left = jnp.concatenate([part[flip] for part in (own, pair, far, both)], axis=0)
        ref[...] = dot(left, live, ((1,), (1,))).reshape(ref.shape)


def act_call(lens, own, pair, far, both, vals):
    rows, piece = own.shape[1:]
    shape = jax.ShapeDtypeStruct((2, 2, rows, LIVE), jnp.float32)
    count = 8 * rows
    return pl.pallas_call(
        act_kernel,
        out_shape=(shape, shape),
        in_specs=[SMEM] + [VMEM] * 5,
        out_specs=(VMEM, VMEM),
        compiler_params=params(),
        cost_estimate=cost(2 * (count + SLOTS) * LIVE * piece, 4 * SLOTS * piece + 4 * count * LIVE),
    )(lens, own, pair, far, both, vals)


def combine_kernel(spot, ids, own, pair, away, both, grads, scale, out):
    depth, _, rows, _ = grads.shape
    per = 128 // rows
    row = lax.broadcasted_iota(jnp.int32, (8, 128), 0)
    lane = lax.broadcasted_iota(jnp.int32, (8, 128), 1)
    seqs = lax.broadcasted_iota(jnp.int32, (8, rows), 0)
    sums = jnp.zeros((8, 128), jnp.float32)
    for far in range(2):
        number = far * depth + spot[3]
        lanes = ids[:, pl.ds(pl.multiple_of((number // per) * 128, 128), 128)]
        owner = lanes[:, :rows]
        for turn in range(1, per):
            owner = jnp.where(number % per == turn, lanes[:, turn * rows : (turn + 1) * rows], owner)
        flip = spot[2] ^ far
        act = own[flip] + pair[flip] + away[1 - flip] + both[1 - flip]
        folded = []
        for other in range(depth):
            code = grads[other, far].astype(jnp.int32).astype(jnp.float32)
            terms = act * (code * jnp.abs(code))
            folded.append(sum(terms[:, at : at + 128] for at in range(0, LIVE, 128)))
        held = lax.dot_general(
            jnp.where(seqs == owner, 1.0, 0.0), jnp.concatenate(folded, axis=1), (((1,), (0,)), ((), ())),
            precision=lax.Precision.HIGHEST, preferred_element_type=jnp.float32,
        )
        for other in range(depth):
            column = jnp.sum(held[:, other * 128 : (other + 1) * 128], axis=1, keepdims=True)
            sums = jnp.where(lane // SEQ_DEV == far * depth + other, column, sums)
    place = lane % 64
    value = jnp.where((row == lane % SEQ_DEV) & (lane < 64), sums, 0.0)
    block = jnp.where(place // (SEQ_DEV * depth) == 0, scale[0:8], scale[8:16])
    mine = (row == 0) & (lane >= 64) & (place // SEQ_DEV % depth == spot[3])
    out[...] = jnp.sum(jnp.where(mine, block, value), axis=0, keepdims=True)


def combine_call(spot, ids, acts, grads, scale):
    return pl.pallas_call(
        combine_kernel,
        out_shape=jax.ShapeDtypeStruct((1, 128), jnp.float32),
        in_specs=[SMEM] + [VMEM] * 7,
        out_specs=VMEM,
        compiler_params=params(),
        cost_estimate=cost(4 * grads.size, 4 * grads.size),
    )(spot, ids, *acts, grads, scale)


def total_kernel(depth, norm, terms, out):
    count = terms.shape[0]
    groups = jnp.sum(terms[...].reshape(count // depth, depth, 128), axis=1)
    lane = lax.broadcasted_iota(jnp.int32, groups.shape, 1)
    scaled = jnp.where(lane < 64, groups * pltpu.roll(groups, 64, 1), 0.0)
    whole = jnp.sum(scaled, axis=0, keepdims=True)
    lane = lax.broadcasted_iota(jnp.int32, whole.shape, 1)
    scores = [
        jnp.sum(jnp.where(lane % SEQ_DEV == seq, whole, 0.0), axis=1, keepdims=True) for seq in range(SEQ_DEV)
    ]
    out[...] = jnp.concatenate(scores, axis=1) * (norm / (CODES * CODES))


def on_device(train_act, train_grad, val_act, val_grad, segment_ids, val_lengths):
    tok_count = segment_ids.shape[1]
    rows, width = train_act.shape[1:]
    val_rows = val_act.shape[1]
    parts = lax.axis_size(SLICES)
    depth = lax.axis_size("depth")
    piece = width // parts
    pair, core, far, deep = (lax.axis_index(name) for name in PLANE)
    spot = jnp.stack([pair, core, far, deep]).astype(jnp.int32)

    own = val_grad[0].T
    across = swap(own, "pair")
    later, across = lax.optimization_barrier((spot, across))
    corner = swap(across, "core")
    beside = swap(beside_call(later, own, train_act[0]), "core")

    vals = trade(spread_call(val_act[0], piece, parts * depth), ACROSS).reshape(SLOTS, piece)
    mine, to_pair, to_far, to_both = slices_call(spot, train_act[0], beside, piece)
    parts_in = (mine, swap(to_pair, "pair"), swap(to_far, "far"), swap_both(to_both))

    grad_part, scale = grad_call(spot, val_lengths, (own, beside, across, corner), train_grad[0].T, rows)
    grad_part, *parts_in = lax.optimization_barrier((grad_part, *parts_in))
    grads = trade(grad_part, "depth")

    act_away, act_keep = act_call(val_lengths, *parts_in, vals)
    halves = act_keep + swap(act_away, "core")
    mine, other = halves[:, 0], halves[:, 1]
    acts = (mine, swap(other, "pair"), swap(mine, "far"), swap_both(other))

    terms = combine_call(spot, segment_ids, acts, grads, scale)
    everyone = lax.axis_size(LAYERS)
    terms = trade(jnp.broadcast_to(terms[None], (everyone, 1, 128)), LAYERS).reshape(everyone, 128)
    norm = (tok_count * SLOTS * lax.axis_size("section")) ** -0.5
    return pl.pallas_call(
        functools.partial(total_kernel, depth, norm),
        out_shape=jax.ShapeDtypeStruct((1, SEQ_DEV), jnp.float32),
        in_specs=[VMEM],
        out_specs=VMEM,
        compiler_params=params(),
    )(terms)


def solution(mesh):
    split = Mesh(mesh.devices.reshape(SHAPE), NAMES)
    placed = (
        P("section", PLANE, None),
        P("section", ("pair", "core"), TENSOR),
        P("section", PLANE, None),
        P("section", ("pair", "core"), TENSOR),
        P(("pair", "core"), None),
        P(),
    )
    return jax.shard_map(
        on_device, mesh=split, in_specs=placed, out_specs=P(("pair", "core"), None), check_vma=False
    )
```

time: 115 us -> 107 us (0.930)
  waiting for transfers between devices: 25.4 us -> 12.7 us
  Pallas kernels: 9.77 us -> 12.1 us
  other arithmetic: 2.25 us -> 0.12 us
  blocking collectives: 25.6 us -> 27.7 us
  starting transfers between devices: 48.4 us -> 50.2 us
  local copies, waits for them, and re-layouts: 1.93 us -> 3.08 us
    ppermute x9 -> x8, waiting for transfers between devices: 22.3 us -> 4.55 us  [swap(): return lax.ppermute(value, axis, [(0, 1), (1, 0)])]
    ppermute x0 -> x2, waiting for transfers between devices: none -> 8.07 us  [swap_both(): lax.ppermute(value, ('pair', 'far'), [(0, 3), (1, 2), (2, 1), (3, 0)])]
    ppermute x0 -> x2, starting transfers between devices: none -> 5.62 us  [swap_both(): lax.ppermute(value, ('pair', 'far'), [(0, 3), (1, 2), (2, 1), (3, 0)])]
    ppermute x9 -> x8, starting transfers between devices: 28.1 us -> 24.7 us  [swap(): return lax.ppermute(value, axis, [(0, 1), (1, 0)])]
    unnamed x8 -> x10, local copies, waits for them, and re-layouts: 0.02 us -> 2.99 us
    all_to_all x2, waiting for transfers between devices: 3.06 us -> 0.12 us  [trade(): return lax.all_to_all(value, axes, 0, 0, tiled=True)]
    all_to_all x1, blocking collectives: 25.6 us -> 27.7 us  [trade(): return lax.all_to_all(value, axes, 0, 0, tiled=True)]
    pallas_call x4 -> x6, Pallas kernels: 8.8 us -> 10.8 us  [the longest x1 6.35 us: grad_call(): pl.pallas_call(grad_kernel, out_shape=(jax.ShapeDtypeStruct((toks // (2 *...]
  transfers between devices with their start and end apart: 11 -> 12, of which waited for: 6 -> 5; matrix products, arithmetic and copies ran while one was open for 4% -> 0% of each run, Pallas kernels for 7% -> 10%
where the time goes in v3:
time: 107 us; the launch traced here: 106 us
  starting transfers between devices  50.2 us (47%)
  blocking collectives  27.7 us (26%)
  waiting for transfers between devices  12.7 us (12%)
  Pallas kernels  12.1 us (11%)
  local copies, waits for them, and re-layouts  3.08 us (3%)
    all_to_all x1, blocking collectives, trade(): return lax.all_to_all(value, axes, 0, 0, tiled=True)  27.7 us
    ppermute x8, starting transfers between devices, swap(): return lax.ppermute(value, axis, [(0, 1), (1, 0)])  24.7 us
    all_to_all x2, starting transfers between devices, trade(): return lax.all_to_all(value, axes, 0, 0, tiled=True)  19.9 us
    ppermute x2, waiting for transfers between devices, swap_both(): lax.ppermute(value, ('pair', 'far'), [(0, 3), (1, 2), (2, 1), (3, 0)])  8.07 us
    pallas_call x1, Pallas kernels, grad_call(): pl.pallas_call(grad_kernel, out_shape=(jax.ShapeDtypeStruct((toks // (2 *...  6.35 us
    ppermute x2, starting transfers between devices, swap_both(): lax.ppermute(value, ('pair', 'far'), [(0, 3), (1, 2), (2, 1), (3, 0)])  5.62 us
    ppermute x8, waiting for transfers between devices, swap(): return lax.ppermute(value, axis, [(0, 1), (1, 0)])  4.55 us
    unnamed x10, local copies, waits for them, and re-layouts  2.99 us
  transfers between devices with their start and end apart: 12, of which 5 were waited for; matrix products, arithmetic and copies ran while one was open for 0% of the time, Pallas kernels for 10%

profile of v3, /device:TPU:1, one launch (start us, length us, event | category | flops | bytes accessed | tf_op | source)
XLA Modules:
  0.0 106.1 jit_solution(339129050886813623)
XLA Ops:
  0.0 0.0 copy-start.4
  0.0 4.1 %collective-permute-start = (bf16[1728,128]{1,0:T(8,128)(2,1)}, bf16[1728,128]{1,0:T(8,128)(2,1)S(1)}, u32[]{:S(2)}, u32[]{:S(2)}) collective-permute-start(bf16[1728,128]{1,0:T(8,128)(2,1)} %bitcast.21), channel_id=1, source_target_pairs={{0,32},{32,0},{1,33},{33,1},{2,34},{34,2},{3,35},{35,3},{4,36},{36... | collective-permute-start | bytes 1327112 | tf_op jit(solution)/shard_map/ppermute | solution.py:30
  4.1 0.0 copy-start.2
  4.1 0.9 copy-done.2
  5.0 0.9 shard_map.67
  5.9 14.1 %all-to-all-start = ((bf16[64,8,640]{2,1,0:T(8,128)(2,1)}), bf16[64,8,640]{2,1,0:T(8,128)(2,1)S(1)}, u32[]{:S(2)}, u32[]{:S(2)}) async-start(bf16[64,8,640]{2,1,0:T(8,128)(2,1)} %shard_map.67), calls=%async_computation | async-start | bytes 1310720 | tf_op jit(solution)/shard_map/all_to_all | solution.py:38
  20.0 0.1 pad_add_fusion.spot
  20.1 0.0 collective-permute-done.across
  20.1 0.0 copy-start
  20.1 1.1 %copy-done = bf16[1,64,5120]{2,1,0:T(8,128)(2,1)S(1)} copy-done((bf16[1,64,5120]{2,1,0:T(8,128)(2,1)S(1)}, bf16[1,64,5120]{2,1,0:T(8,128)(2,1)}, u32[]{:S(2)}) %copy-start) | copy-done | bytes 655384
  21.2 0.0 copy-start.1
  21.2 1.0 copy-done.1
  22.2 0.7 shard_map.64
  22.9 2.3 %collective-permute-start.1 = (bf16[3008,128]{1,0:T(8,128)(2,1)S(1)}, bf16[3008,128]{1,0:T(8,128)(2,1)S(1)}, u32[]{:S(2)}, u32[]{:S(2)}) collective-permute-start(bf16[3008,128]{1,0:T(8,128)(2,1)S(1)} %shard_map.64), channel_id=1, source_target_pairs={{0,16},{16,0},{1,17},{17,1},{2,18},{18,2},{3,19},{19,3},{4,20},{20... | collective-permute-start | bytes 2310152 | tf_op jit(solution)/shard_map/ppermute | solution.py:30
  25.1 2.1 %collective-permute-start.2 = (bf16[1728,128]{1,0:T(8,128)(2,1)S(1)}, bf16[1728,128]{1,0:T(8,128)(2,1)S(1)}, u32[]{:S(2)}, u32[]{:S(2)}) collective-permute-start(bf16[1728,128]{1,0:T(8,128)(2,1)S(1)} %collective-permute-done.across), channel_id=1, source_target_pairs={{0,16},{16,0},{1,17},{17,1},{2,18},{18,2},{3,19},{19,3},{4,20},{20... | collective-permute-start | bytes 1327112 | tf_op jit(solution)/shard_map/ppermute | solution.py:30
  27.2 0.0 collective-permute-done.1.beside.got
  27.2 0.6 shard_map.66
  27.9 3.4 %collective-permute-start.3 = (bf16[2,64,640]{2,1,0:T(8,128)(2,1)S(1)}, bf16[2,64,640]{2,1,0:T(8,128)(2,1)S(1)}, u32[]{:S(2)}, u32[]{:S(2)}) collective-permute-start(bf16[2,64,640]{2,1,0:T(8,128)(2,1)S(1)} %get-tuple-element.24), channel_id=1, source_target_pairs={{0,32},{32,0},{1,33},{33,1},{2,34},{34,2},{3,35},{35,3},{4,36},{36... | collective-permute-start | bytes 491528 | tf_op jit(solution)/shard_map/ppermute | solution.py:30
  31.2 4.4 %collective-permute-start.4 = (bf16[2,64,640]{2,1,0:T(8,128)(2,1)S(1)}, bf16[2,64,640]{2,1,0:T(8,128)(2,1)S(1)}, u32[]{:S(2)}, u32[]{:S(2)}) collective-permute-start(bf16[2,64,640]{2,1,0:T(8,128)(2,1)S(1)} %get-tuple-element.25), channel_id=1, source_target_pairs={{0,8},{8,0},{1,9},{9,1},{2,10},{10,2},{3,11},{11,3},{4,12},{12,4},... | collective-permute-start | bytes 491528 | tf_op jit(solution)/shard_map/ppermute | solution.py:30
  35.6 1.9 %collective-permute-start.5 = (bf16[2,64,640]{2,1,0:T(8,128)(2,1)S(1)}, bf16[2,64,640]{2,1,0:T(8,128)(2,1)S(1)}, u32[]{:S(2)}, u32[]{:S(2)}) collective-permute-start(bf16[2,64,640]{2,1,0:T(8,128)(2,1)S(1)} %get-tuple-element.26), channel_id=1, source_target_pairs={{0,40},{8,32},{32,8},{40,0},{1,41},{9,33},{33,9},{41,1},{2,42},{10... | collective-permute-start | bytes 491528 | tf_op jit(solution)/shard_map/ppermute | solution.py:34
  37.5 0.0 collective-permute-done.2.corner
  37.5 0.0 copy-done.4
  37.6 6.3 %shard_map.65 = (s16[8,2,64,384]{3,2,1,0:T(8,128)(2,1)}, f32[16,128]{1,0:T(8,128)S(1)}) custom-call(s32[4]{0:T(128)S(1)} %pad_add_fusion.spot, s32[8]{0:T(128)S(1)} %copy-done.4, bf16[1728,128]{1,0:T(8,128)(2,1)S(1)} %bitcast.23, bf16[3008,128]{1,0:T(8,128)(2,1)S(1)} %collective-permute-done.1.beside.got, bf16[1728,128]{1,0:T(8,128)(2,1)S(1)} %collective-permute-done.across, ...), custom_call_target="tpu_custom_call" | custom-call | flops 1358954496 | bytes 5111808 | tf_op jit(solution)/shard_map/pallas_call | solution.py:163
  43.9 0.0 copy-start.3
  43.9 0.0 collective-permute-done.3.pair
  43.9 0.0 collective-permute-done.4.far
  43.9 3.1 %collective-permute-done.5.both = bf16[2,64,640]{2,1,0:T(8,128)(2,1)S(1)} collective-permute-done((bf16[2,64,640]{2,1,0:T(8,128)(2,1)S(1)}, bf16[2,64,640]{2,1,0:T(8,128)(2,1)S(1)}, u32[]{:S(2)}, u32[]{:S(2)}) %collective-permute-start.5) | collective-permute-done | bytes 163872 | tf_op jit(solution)/shard_map/ppermute | solution.py:34
  47.1 0.0 all-to-all-done
  47.1 5.8 %all-to-all-start.1 = ((s16[8,2,64,384]{3,2,1,0:T(8,128)(2,1)}), s16[8,2,64,384]{3,2,1,0:T(8,128)(2,1)S(1)}, u32[]{:S(2)}, u32[]{:S(2)}) async-start(s16[8,2,64,384]{3,2,1,0:T(8,128)(2,1)} %get-tuple-element.33), calls=%async_computation.1 | async-start | bytes 1572864 | tf_op jit(solution)/shard_map/all_to_all | solution.py:38
  52.8 1.6 %shard_map.68 = (f32[2,2,64,384]{3,2,1,0:T(8,128)S(1)}, f32[2,2,64,384]{3,2,1,0:T(8,128)S(1)}) custom-call(s32[8]{0:T(128)S(1)} %copy-done.4, bf16[2,64,640]{2,1,0:T(8,128)(2,1)S(1)} %get-tuple-element.27.own, bf16[2,64,640]{2,1,0:T(8,128)(2,1)S(1)} %collective-permute-done.3.pair, bf16[2,64,640]{2,1,0:T(8,128)(2,1)S(1)} %collective-permute-done.4.far, ...), custom_call_target="tpu_custom_call" | custom-call | flops 503316480 | bytes 2097152 | tf_op jit(solution)/shard_map/pallas_call | solution.py:192
  54.5 2.7 %collective-permute-start.6 = (f32[2,2,64,384]{3,2,0,1:T(8,128)S(1)}, f32[2,2,64,384]{3,2,0,1:T(8,128)S(1)}, u32[]{:S(2)}, u32[]{:S(2)}) collective-permute-start(f32[2,2,64,384]{3,2,0,1:T(8,128)S(1)} %copy.9), channel_id=1, source_target_pairs={{0,16},{16,0},{1,17},{17,1},{2,18},{18,2},{3,19},{19,3},{4,20},{20... | collective-permute-start | bytes 1179656 | tf_op jit(solution)/shard_map/ppermute | solution.py:30
  57.1 1.3 %collective-permute-done.6 = f32[2,2,64,384]{3,2,0,1:T(8,128)S(1)} collective-permute-done((f32[2,2,64,384]{3,2,0,1:T(8,128)S(1)}, f32[2,2,64,384]{3,2,0,1:T(8,128)S(1)}, u32[]{:S(2)}, u32[]{:S(2)}) %collective-permute-start.6) | collective-permute-done | bytes 393248 | tf_op jit(solution)/shard_map/ppermute | solution.py:30
  58.6 1.9 %collective-permute-start.7 = (f32[2,64,384]{2,1,0:T(8,128)S(1)}, f32[2,64,384]{2,1,0:T(8,128)S(1)}, u32[]{:S(2)}, u32[]{:S(2)}) collective-permute-start(f32[2,64,384]{2,1,0:T(8,128)S(1)} %get-tuple-element.35), channel_id=1, source_target_pairs={{0,32},{32,0},{1,33},{33,1},{2,34},{34,2},{3,35},{35,3},{4,36},{36... | collective-permute-start | bytes 589832 | tf_op jit(solution)/shard_map/ppermute | solution.py:30
  60.5 4.0 %collective-permute-start.8 = (f32[2,64,384]{2,1,0:T(8,128)S(1)}, f32[2,64,384]{2,1,0:T(8,128)S(1)}, u32[]{:S(2)}, u32[]{:S(2)}) collective-permute-start(f32[2,64,384]{2,1,0:T(8,128)S(1)} %get-tuple-element.36.own), channel_id=1, source_target_pairs={{0,8},{8,0},{1,9},{9,1},{2,10},{10,2},{3,11},{11,3},{4,12},{12,4},... | collective-permute-start | bytes 589832 | tf_op jit(solution)/shard_map/ppermute | solution.py:30
  64.5 3.7 %collective-permute-start.9 = (f32[2,64,384]{2,1,0:T(8,128)S(1)}, f32[2,64,384]{2,1,0:T(8,128)S(1)}, u32[]{:S(2)}, u32[]{:S(2)}) collective-permute-start(f32[2,64,384]{2,1,0:T(8,128)S(1)} %get-tuple-element.35), channel_id=1, source_target_pairs={{0,40},{8,32},{32,8},{40,0},{1,41},{9,33},{33,9},{41,1},{2,42},{10... | collective-permute-start | bytes 589832 | tf_op jit(solution)/shard_map/ppermute | solution.py:34
  68.2 0.0 collective-permute-done.7.pair
  68.2 3.2 %collective-permute-done.8.away = f32[2,64,384]{2,1,0:T(8,128)S(1)} collective-permute-done((f32[2,64,384]{2,1,0:T(8,128)S(1)}, f32[2,64,384]{2,1,0:T(8,128)S(1)}, u32[]{:S(2)}, u32[]{:S(2)}) %collective-permute-start.8) | collective-permute-done | bytes 196640 | tf_op jit(solution)/shard_map/ppermute | solution.py:30
  71.4 4.9 %collective-permute-done.9.both = f32[2,64,384]{2,1,0:T(8,128)S(1)} collective-permute-done((f32[2,64,384]{2,1,0:T(8,128)S(1)}, f32[2,64,384]{2,1,0:T(8,128)S(1)}, u32[]{:S(2)}, u32[]{:S(2)}) %collective-permute-start.9) | collective-permute-done | bytes 196640 | tf_op jit(solution)/shard_map/ppermute | solution.py:34
  76.3 0.1 all-to-all-done.1.grads
  76.4 0.0 copy-done.3
  76.4 1.2 %shard_map.69 = f32[1,128]{1,0:T(1,128)S(1)} custom-call(s32[4]{0:T(128)S(1)} %pad_add_fusion.spot, s32[1,1024]{1,0:T(1,128)S(1)} %copy-done.3, f32[2,64,384]{2,1,0:T(8,128)S(1)} %get-tuple-element.36.own, f32[2,64,384]{2,1,0:T(8,128)S(1)} %collective-permute-done.7.pair, f32[2,64,384]{2,1,0:T(8,128)S(1)} %collective-permute-done.8.away, ...), custom_call_target="tpu_custom_call" | custom-call | flops 1572864 | bytes 1572864 | tf_op jit(solution)/shard_map/pallas_call | solution.py:237
  77.7 27.7 %all_to_all.15 = f32[128,1,128]{2,1,0:T(1,128)S(1)} all-to-all(f32[128,1,128]{2,1,0:T(1,128)S(1)} %broadcast_in_dim.9), channel_id=1, replica_groups=mesh['section'=8,'pair'=2,'core'=2,'far'=2,'depth'=8] {'section','far','..., dimensions={0} | all-to-all | bytes 131072 | tf_op jit(solution)/shard_map/all_to_all | solution.py:38
  105.4 0.7 shard_map.70
  (4 shorter events, 0.1 us)
Async XLA Ops:
  0.0 37.5 %copy-start.4 = (s32[8]{0:T(128)S(1)}, s32[8]{0:T(128)}, u32[]{:S(2)}) copy-start(s32[8]{0:T(128)} %lens.3) | copy-start | bytes 100
  0.0 20.1 %collective-permute-start = (bf16[1728,128]{1,0:T(8,128)(2,1)}, bf16[1728,128]{1,0:T(8,128)(2,1)S(1)}, u32[]{:S(2)}, u32[]{:S(2)}) collective-permute-start(bf16[1728,128]{1,0:T(8,128)(2,1)} %bitcast.21), channel_id=1, source_target_pairs={{0,32},{32,0},{1,33},{33,1},{2,34},{34,2},{3,35},{35,3},{4,36},{36... | collective-permute-start | bytes 1327112 | tf_op jit(solution)/shard_map/ppermute | solution.py:30
  4.1 0.9 copy-start.2
  5.9 41.2 %all-to-all-start = ((bf16[64,8,640]{2,1,0:T(8,128)(2,1)}), bf16[64,8,640]{2,1,0:T(8,128)(2,1)S(1)}, u32[]{:S(2)}, u32[]{:S(2)}) async-start(bf16[64,8,640]{2,1,0:T(8,128)(2,1)} %shard_map.67), calls=%async_computation | async-start | bytes 1310720 | tf_op jit(solution)/shard_map/all_to_all | solution.py:38
  20.1 1.1 %copy-start = (bf16[1,64,5120]{2,1,0:T(8,128)(2,1)S(1)}, bf16[1,64,5120]{2,1,0:T(8,128)(2,1)}, u32[]{:S(2)}) copy-start(bf16[1,64,5120]{2,1,0:T(8,128)(2,1)} %param.6) | copy-start | bytes 1966084
  21.2 1.0 copy-start.1
  22.9 4.3 %collective-permute-start.1 = (bf16[3008,128]{1,0:T(8,128)(2,1)S(1)}, bf16[3008,128]{1,0:T(8,128)(2,1)S(1)}, u32[]{:S(2)}, u32[]{:S(2)}) collective-permute-start(bf16[3008,128]{1,0:T(8,128)(2,1)S(1)} %shard_map.64), channel_id=1, source_target_pairs={{0,16},{16,0},{1,17},{17,1},{2,18},{18,2},{3,19},{19,3},{4,20},{20... | collective-permute-start | bytes 2310152 | tf_op jit(solution)/shard_map/ppermute | solution.py:30
  25.1 12.4 %collective-permute-start.2 = (bf16[1728,128]{1,0:T(8,128)(2,1)S(1)}, bf16[1728,128]{1,0:T(8,128)(2,1)S(1)}, u32[]{:S(2)}, u32[]{:S(2)}) collective-permute-start(bf16[1728,128]{1,0:T(8,128)(2,1)S(1)} %collective-permute-done.across), channel_id=1, source_target_pairs={{0,16},{16,0},{1,17},{17,1},{2,18},{18,2},{3,19},{19,3},{4,20},{20... | collective-permute-start | bytes 1327112 | tf_op jit(solution)/shard_map/ppermute | solution.py:30
  27.9 16.0 %collective-permute-start.3 = (bf16[2,64,640]{2,1,0:T(8,128)(2,1)S(1)}, bf16[2,64,640]{2,1,0:T(8,128)(2,1)S(1)}, u32[]{:S(2)}, u32[]{:S(2)}) collective-permute-start(bf16[2,64,640]{2,1,0:T(8,128)(2,1)S(1)} %get-tuple-element.24), channel_id=1, source_target_pairs={{0,32},{32,0},{1,33},{33,1},{2,34},{34,2},{3,35},{35,3},{4,36},{36... | collective-permute-start | bytes 491528 | tf_op jit(solution)/shard_map/ppermute | solution.py:30
  31.2 12.7 %collective-permute-start.4 = (bf16[2,64,640]{2,1,0:T(8,128)(2,1)S(1)}, bf16[2,64,640]{2,1,0:T(8,128)(2,1)S(1)}, u32[]{:S(2)}, u32[]{:S(2)}) collective-permute-start(bf16[2,64,640]{2,1,0:T(8,128)(2,1)S(1)} %get-tuple-element.25), channel_id=1, source_target_pairs={{0,8},{8,0},{1,9},{9,1},{2,10},{10,2},{3,11},{11,3},{4,12},{12,4},... | collective-permute-start | bytes 491528 | tf_op jit(solution)/shard_map/ppermute | solution.py:30
  35.6 11.5 %collective-permute-start.5 = (bf16[2,64,640]{2,1,0:T(8,128)(2,1)S(1)}, bf16[2,64,640]{2,1,0:T(8,128)(2,1)S(1)}, u32[]{:S(2)}, u32[]{:S(2)}) collective-permute-start(bf16[2,64,640]{2,1,0:T(8,128)(2,1)S(1)} %get-tuple-element.26), channel_id=1, source_target_pairs={{0,40},{8,32},{32,8},{40,0},{1,41},{9,33},{33,9},{41,1},{2,42},{10... | collective-permute-start | bytes 491528 | tf_op jit(solution)/shard_map/ppermute | solution.py:34
  43.9 32.5 %copy-start.3 = (s32[1,1024]{1,0:T(1,128)S(1)}, s32[1,1024]{1,0:T(1,128)}, u32[]{:S(2)}) copy-start(s32[1,1024]{1,0:T(1,128)} %ids.1) | copy-start | bytes 12292
  47.1 29.4 %all-to-all-start.1 = ((s16[8,2,64,384]{3,2,1,0:T(8,128)(2,1)}), s16[8,2,64,384]{3,2,1,0:T(8,128)(2,1)S(1)}, u32[]{:S(2)}, u32[]{:S(2)}) async-start(s16[8,2,64,384]{3,2,1,0:T(8,128)(2,1)} %get-tuple-element.33), calls=%async_computation.1 | async-start | bytes 1572864 | tf_op jit(solution)/shard_map/all_to_all | solution.py:38
  54.5 4.0 %collective-permute-start.6 = (f32[2,2,64,384]{3,2,0,1:T(8,128)S(1)}, f32[2,2,64,384]{3,2,0,1:T(8,128)S(1)}, u32[]{:S(2)}, u32[]{:S(2)}) collective-permute-start(f32[2,2,64,384]{3,2,0,1:T(8,128)S(1)} %copy.9), channel_id=1, source_target_pairs={{0,16},{16,0},{1,17},{17,1},{2,18},{18,2},{3,19},{19,3},{4,20},{20... | collective-permute-start | bytes 1179656 | tf_op jit(solution)/shard_map/ppermute | solution.py:30
  58.6 9.6 %collective-permute-start.7 = (f32[2,64,384]{2,1,0:T(8,128)S(1)}, f32[2,64,384]{2,1,0:T(8,128)S(1)}, u32[]{:S(2)}, u32[]{:S(2)}) collective-permute-start(f32[2,64,384]{2,1,0:T(8,128)S(1)} %get-tuple-element.35), channel_id=1, source_target_pairs={{0,32},{32,0},{1,33},{33,1},{2,34},{34,2},{3,35},{35,3},{4,36},{36... | collective-permute-start | bytes 589832 | tf_op jit(solution)/shard_map/ppermute | solution.py:30
  60.5 10.9 %collective-permute-start.8 = (f32[2,64,384]{2,1,0:T(8,128)S(1)}, f32[2,64,384]{2,1,0:T(8,128)S(1)}, u32[]{:S(2)}, u32[]{:S(2)}) collective-permute-start(f32[2,64,384]{2,1,0:T(8,128)S(1)} %get-tuple-element.36.own), channel_id=1, source_target_pairs={{0,8},{8,0},{1,9},{9,1},{2,10},{10,2},{3,11},{11,3},{4,12},{12,4},... | collective-permute-start | bytes 589832 | tf_op jit(solution)/shard_map/ppermute | solution.py:30
  64.5 11.8 %collective-permute-start.9 = (f32[2,64,384]{2,1,0:T(8,128)S(1)}, f32[2,64,384]{2,1,0:T(8,128)S(1)}, u32[]{:S(2)}, u32[]{:S(2)}) collective-permute-start(f32[2,64,384]{2,1,0:T(8,128)S(1)} %get-tuple-element.35), channel_id=1, source_target_pairs={{0,40},{8,32},{32,8},{40,0},{1,41},{9,33},{33,9},{41,1},{2,42},{10... | collective-permute-start | bytes 589832 | tf_op jit(solution)/shard_map/ppermute | solution.py:34

commit v4 on v3

--- a/solution.py
+++ b/solution.py
@@ -81,7 +81,7 @@
         in_specs=[VMEM],
         out_specs=VMEM,
         compiler_params=params(),
-        cost_estimate=cost(0, 2 * count * val.shape[0] * piece),
+        cost_estimate=cost(4_000_000_000, 2 * count * val.shape[0] * piece),
     )(val)
 
 
@@ -269,9 +269,10 @@
 
     own = val_grad[0].T
     across = swap(own, "pair")
-    later, across = lax.optimization_barrier((spot, across))
+    beside = beside_call(spot, own, train_act[0])
+    beside, across = lax.optimization_barrier((beside, across))
     corner = swap(across, "core")
-    beside = swap(beside_call(later, own, train_act[0]), "core")
+    beside = swap(beside, "core")
 
     vals = trade(spread_call(val_act[0], piece, parts * depth), ACROSS).reshape(SLOTS, piece)
     mine, to_pair, to_far, to_both = slices_call(spot, train_act[0], beside, piece)
@@ -279,9 +280,9 @@
 
     grad_part, scale = grad_call(spot, val_lengths, (own, beside, across, corner), train_grad[0].T, rows)
     grad_part, *parts_in = lax.optimization_barrier((grad_part, *parts_in))
+    act_away, act_keep = act_call(val_lengths, *parts_in, vals)
+    grad_part, act_away = lax.optimization_barrier((grad_part, act_away))
     grads = trade(grad_part, "depth")
-
-    act_away, act_keep = act_call(val_lengths, *parts_in, vals)
     halves = act_keep + swap(act_away, "core")
     mine, other = halves[:, 0], halves[:, 1]
     acts = (mine, swap(other, "pair"), swap(mine, "far"), swap_both(other))

time: 107 us -> 106 us (level)
  waiting for transfers between devices: 12.7 us -> 15.7 us
  local copies, waits for them, and re-layouts: 3.08 us -> 0.99 us
  blocking collectives: 27.7 us -> 26.1 us
    unnamed x10, local copies, waits for them, and re-layouts: 2.99 us -> 0.89 us
    all_to_all x2, waiting for transfers between devices: 0.12 us -> 1.99 us  [trade(): return lax.all_to_all(value, axes, 0, 0, tiled=True)]
    all_to_all x1, blocking collectives: 27.7 us -> 26.1 us  [trade(): return lax.all_to_all(value, axes, 0, 0, tiled=True)]
  transfers between devices with their start and end apart: 12 -> 12, of which waited for: 5 -> 6; matrix products, arithmetic and copies ran while one was open for 0% -> 0% of each run, Pallas kernels for 10% -> 8%
where the time goes in v4:
time: 106 us; the launch traced here: 105 us
  starting transfers between devices  49.7 us (47%)
  blocking collectives  26.1 us (25%)
  waiting for transfers between devices  15.7 us (15%)
  Pallas kernels  12.1 us (11%)
    all_to_all x1, blocking collectives, trade(): return lax.all_to_all(value, axes, 0, 0, tiled=True)  26.1 us
    ppermute x8, starting transfers between devices, swap(): return lax.ppermute(value, axis, [(0, 1), (1, 0)])  24.3 us
    all_to_all x2, starting transfers between devices, trade(): return lax.all_to_all(value, axes, 0, 0, tiled=True)  19.6 us
    ppermute x2, waiting for transfers between devices, swap_both(): lax.ppermute(value, ('pair', 'far'), [(0, 3), (1, 2), (2, 1), (3, 0)])  8.49 us
    pallas_call x1, Pallas kernels, grad_call(): pl.pallas_call(grad_kernel, out_shape=(jax.ShapeDtypeStruct((toks // (2 *...  6.34 us
    ppermute x2, starting transfers between devices, swap_both(): lax.ppermute(value, ('pair', 'far'), [(0, 3), (1, 2), (2, 1), (3, 0)])  5.86 us
    ppermute x8, waiting for transfers between devices, swap(): return lax.ppermute(value, axis, [(0, 1), (1, 0)])  5.23 us
  transfers between devices with their start and end apart: 12, of which 6 were waited for; matrix products, arithmetic and copies ran while one was open for 0% of the time, Pallas kernels for 8%

profile of v4, /device:TPU:1, one launch (start us, length us, event | category | flops | bytes accessed | tf_op | source)
XLA Modules:
  0.0 104.9 jit_solution(5418554608003482921)
XLA Ops:
  0.0 3.9 %collective-permute-start = (bf16[1728,128]{1,0:T(8,128)(2,1)}, bf16[1728,128]{1,0:T(8,128)(2,1)S(1)}, u32[]{:S(2)}, u32[]{:S(2)}) collective-permute-start(bf16[1728,128]{1,0:T(8,128)(2,1)} %bitcast.21), channel_id=1, source_target_pairs={{0,32},{32,0},{1,33},{33,1},{2,34},{34,2},{3,35},{35,3},{4,36},{36... | collective-permute-start | bytes 1327112 | tf_op jit(solution)/shard_map/ppermute | solution.py:30
  3.9 0.0 copy-start.4
  4.0 0.9 copy-done.4
  4.8 0.0 copy-start
  4.8 0.0 copy-start.1
  4.8 0.9 shard_map.67
  5.8 0.0 copy-start.3
  5.8 14.2 %all-to-all-start = ((bf16[64,8,640]{2,1,0:T(8,128)(2,1)}), bf16[64,8,640]{2,1,0:T(8,128)(2,1)S(1)}, u32[]{:S(2)}, u32[]{:S(2)}) async-start(bf16[64,8,640]{2,1,0:T(8,128)(2,1)} %shard_map.67), calls=%async_computation | async-start | bytes 1310720 | tf_op jit(solution)/shard_map/all_to_all | solution.py:38
  20.0 0.1 pad_add_fusion.spot
  20.1 0.0 copy-done
  20.1 0.0 copy-done.1
  20.1 0.7 shard_map.64
  20.8 0.0 collective-permute-done.across
  20.8 2.3 %collective-permute-start.1 = (bf16[3008,128]{1,0:T(8,128)(2,1)S(1)}, bf16[3008,128]{1,0:T(8,128)(2,1)S(1)}, u32[]{:S(2)}, u32[]{:S(2)}) collective-permute-start(bf16[3008,128]{1,0:T(8,128)(2,1)S(1)} %shard_map.64), channel_id=1, source_target_pairs={{0,16},{16,0},{1,17},{17,1},{2,18},{18,2},{3,19},{19,3},{4,20},{20... | collective-permute-start | bytes 2310152 | tf_op jit(solution)/shard_map/ppermute | solution.py:30
  23.1 2.1 %collective-permute-start.2 = (bf16[1728,128]{1,0:T(8,128)(2,1)S(1)}, bf16[1728,128]{1,0:T(8,128)(2,1)S(1)}, u32[]{:S(2)}, u32[]{:S(2)}) collective-permute-start(bf16[1728,128]{1,0:T(8,128)(2,1)S(1)} %collective-permute-done.across), channel_id=1, source_target_pairs={{0,16},{16,0},{1,17},{17,1},{2,18},{18,2},{3,19},{19,3},{4,20},{20... | collective-permute-start | bytes 1327112 | tf_op jit(solution)/shard_map/ppermute | solution.py:30
  25.1 0.0 collective-permute-done.1.beside.got
  25.1 0.6 shard_map.66
  25.8 3.4 %collective-permute-start.3 = (bf16[2,64,640]{2,1,0:T(8,128)(2,1)S(1)}, bf16[2,64,640]{2,1,0:T(8,128)(2,1)S(1)}, u32[]{:S(2)}, u32[]{:S(2)}) collective-permute-start(bf16[2,64,640]{2,1,0:T(8,128)(2,1)S(1)} %get-tuple-element.26), channel_id=1, source_target_pairs={{0,32},{32,0},{1,33},{33,1},{2,34},{34,2},{3,35},{35,3},{4,36},{36... | collective-permute-start | bytes 491528 | tf_op jit(solution)/shard_map/ppermute | solution.py:30
  29.2 4.4 %collective-permute-start.4 = (bf16[2,64,640]{2,1,0:T(8,128)(2,1)S(1)}, bf16[2,64,640]{2,1,0:T(8,128)(2,1)S(1)}, u32[]{:S(2)}, u32[]{:S(2)}) collective-permute-start(bf16[2,64,640]{2,1,0:T(8,128)(2,1)S(1)} %get-tuple-element.27), channel_id=1, source_target_pairs={{0,8},{8,0},{1,9},{9,1},{2,10},{10,2},{3,11},{11,3},{4,12},{12,4},... | collective-permute-start | bytes 491528 | tf_op jit(solution)/shard_map/ppermute | solution.py:30
  33.5 1.9 %collective-permute-start.5 = (bf16[2,64,640]{2,1,0:T(8,128)(2,1)S(1)}, bf16[2,64,640]{2,1,0:T(8,128)(2,1)S(1)}, u32[]{:S(2)}, u32[]{:S(2)}) collective-permute-start(bf16[2,64,640]{2,1,0:T(8,128)(2,1)S(1)} %get-tuple-element.28), channel_id=1, source_target_pairs={{0,40},{8,32},{32,8},{40,0},{1,41},{9,33},{33,9},{41,1},{2,42},{10... | collective-permute-start | bytes 491528 | tf_op jit(solution)/shard_map/ppermute | solution.py:34
  35.4 0.0 collective-permute-done.2.corner
  35.5 0.0 copy-done.3
  35.5 6.3 %shard_map.65 = (s16[8,2,64,384]{3,2,1,0:T(8,128)(2,1)}, f32[16,128]{1,0:T(8,128)S(1)}) custom-call(s32[4]{0:T(128)S(1)} %pad_add_fusion.spot, s32[8]{0:T(128)S(1)} %copy-done.3, bf16[1728,128]{1,0:T(8,128)(2,1)S(1)} %bitcast.23, bf16[3008,128]{1,0:T(8,128)(2,1)S(1)} %collective-permute-done.1.beside.got, bf16[1728,128]{1,0:T(8,128)(2,1)S(1)} %collective-permute-done.across, ...), custom_call_target="tpu_custom_call" | custom-call | flops 1358954496 | bytes 5111808 | tf_op jit(solution)/shard_map/pallas_call | solution.py:163
  41.8 0.0 copy-start.2
  41.8 0.0 collective-permute-done.3.pair
  41.8 0.9 collective-permute-done.4.far
  42.7 3.6 %collective-permute-done.5.both = bf16[2,64,640]{2,1,0:T(8,128)(2,1)S(1)} collective-permute-done((bf16[2,64,640]{2,1,0:T(8,128)(2,1)S(1)}, bf16[2,64,640]{2,1,0:T(8,128)(2,1)S(1)}, u32[]{:S(2)}, u32[]{:S(2)}) %collective-permute-start.5) | collective-permute-done | bytes 163872 | tf_op jit(solution)/shard_map/ppermute | solution.py:34
  46.3 0.0 all-to-all-done
  46.3 1.6 %shard_map.68 = (f32[2,2,64,384]{3,2,1,0:T(8,128)S(1)}, f32[2,2,64,384]{3,2,1,0:T(8,128)S(1)}) custom-call(s32[8]{0:T(128)S(1)} %copy-done.3, bf16[2,64,640]{2,1,0:T(8,128)(2,1)S(1)} %get-tuple-element.29.own, bf16[2,64,640]{2,1,0:T(8,128)(2,1)S(1)} %collective-permute-done.3.pair, bf16[2,64,640]{2,1,0:T(8,128)(2,1)S(1)} %collective-permute-done.4.far, ...), custom_call_target="tpu_custom_call" | custom-call | flops 503316480 | bytes 2097152 | tf_op jit(solution)/shard_map/pallas_call | solution.py:192
  47.9 5.3 %all-to-all-start.1 = ((s16[8,2,64,384]{3,2,1,0:T(8,128)(2,1)}), s16[8,2,64,384]{3,2,1,0:T(8,128)(2,1)S(1)}, u32[]{:S(2)}, u32[]{:S(2)}) async-start(s16[8,2,64,384]{3,2,1,0:T(8,128)(2,1)} %get-tuple-element.37), calls=%async_computation.1 | async-start | bytes 1572864 | tf_op jit(solution)/shard_map/all_to_all | solution.py:38
  53.3 2.6 %collective-permute-start.6 = (f32[2,2,64,384]{3,2,0,1:T(8,128)S(1)}, f32[2,2,64,384]{3,2,0,1:T(8,128)S(1)}, u32[]{:S(2)}, u32[]{:S(2)}) collective-permute-start(f32[2,2,64,384]{3,2,0,1:T(8,128)S(1)} %copy.9), channel_id=1, source_target_pairs={{0,16},{16,0},{1,17},{17,1},{2,18},{18,2},{3,19},{19,3},{4,20},{20... | collective-permute-start | bytes 1179656 | tf_op jit(solution)/shard_map/ppermute | solution.py:30
  55.9 1.3 %collective-permute-done.6 = f32[2,2,64,384]{3,2,0,1:T(8,128)S(1)} collective-permute-done((f32[2,2,64,384]{3,2,0,1:T(8,128)S(1)}, f32[2,2,64,384]{3,2,0,1:T(8,128)S(1)}, u32[]{:S(2)}, u32[]{:S(2)}) %collective-permute-start.6) | collective-permute-done | bytes 393248 | tf_op jit(solution)/shard_map/ppermute | solution.py:30
  57.3 1.9 %collective-permute-start.7 = (f32[2,64,384]{2,1,0:T(8,128)S(1)}, f32[2,64,384]{2,1,0:T(8,128)S(1)}, u32[]{:S(2)}, u32[]{:S(2)}) collective-permute-start(f32[2,64,384]{2,1,0:T(8,128)S(1)} %get-tuple-element.39), channel_id=1, source_target_pairs={{0,32},{32,0},{1,33},{33,1},{2,34},{34,2},{3,35},{35,3},{4,36},{36... | collective-permute-start | bytes 589832 | tf_op jit(solution)/shard_map/ppermute | solution.py:30
  59.2 3.7 %collective-permute-start.8 = (f32[2,64,384]{2,1,0:T(8,128)S(1)}, f32[2,64,384]{2,1,0:T(8,128)S(1)}, u32[]{:S(2)}, u32[]{:S(2)}) collective-permute-start(f32[2,64,384]{2,1,0:T(8,128)S(1)} %get-tuple-element.40.own), channel_id=1, source_target_pairs={{0,8},{8,0},{1,9},{9,1},{2,10},{10,2},{3,11},{11,3},{4,12},{12,4},... | collective-permute-start | bytes 589832 | tf_op jit(solution)/shard_map/ppermute | solution.py:30
  63.0 3.9 %collective-permute-start.9 = (f32[2,64,384]{2,1,0:T(8,128)S(1)}, f32[2,64,384]{2,1,0:T(8,128)S(1)}, u32[]{:S(2)}, u32[]{:S(2)}) collective-permute-start(f32[2,64,384]{2,1,0:T(8,128)S(1)} %get-tuple-element.39), channel_id=1, source_target_pairs={{0,40},{8,32},{32,8},{40,0},{1,41},{9,33},{33,9},{41,1},{2,42},{10... | collective-permute-start | bytes 589832 | tf_op jit(solution)/shard_map/ppermute | solution.py:34
  66.9 0.0 collective-permute-done.7.pair
  66.9 3.0 %collective-permute-done.8.away = f32[2,64,384]{2,1,0:T(8,128)S(1)} collective-permute-done((f32[2,64,384]{2,1,0:T(8,128)S(1)}, f32[2,64,384]{2,1,0:T(8,128)S(1)}, u32[]{:S(2)}, u32[]{:S(2)}) %collective-permute-start.8) | collective-permute-done | bytes 196640 | tf_op jit(solution)/shard_map/ppermute | solution.py:30
  69.9 4.9 %collective-permute-done.9.both = f32[2,64,384]{2,1,0:T(8,128)S(1)} collective-permute-done((f32[2,64,384]{2,1,0:T(8,128)S(1)}, f32[2,64,384]{2,1,0:T(8,128)S(1)}, u32[]{:S(2)}, u32[]{:S(2)}) %collective-permute-start.9) | collective-permute-done | bytes 196640 | tf_op jit(solution)/shard_map/ppermute | solution.py:34
  74.8 2.0 %all-to-all-done.1.grads = s16[8,2,64,384]{3,2,1,0:T(8,128)(2,1)S(1)} async-done(((s16[8,2,64,384]{3,2,1,0:T(8,128)(2,1)}), s16[8,2,64,384]{3,2,1,0:T(8,128)(2,1)S(1)}, u32[]{:S(2)}, u32[]{:S(2)}) %all-to-all-start.1) | async-done | bytes 786464 | tf_op jit(solution)/shard_map/all_to_all | solution.py:38
  76.8 0.0 copy-done.2
  76.8 1.2 %shard_map.69 = f32[1,128]{1,0:T(1,128)S(1)} custom-call(s32[4]{0:T(128)S(1)} %pad_add_fusion.spot, s32[1,1024]{1,0:T(1,128)S(1)} %copy-done.2, f32[2,64,384]{2,1,0:T(8,128)S(1)} %get-tuple-element.40.own, f32[2,64,384]{2,1,0:T(8,128)S(1)} %collective-permute-done.7.pair, f32[2,64,384]{2,1,0:T(8,128)S(1)} %collective-permute-done.8.away, ...), custom_call_target="tpu_custom_call" | custom-call | flops 1572864 | bytes 1572864 | tf_op jit(solution)/shard_map/pallas_call | solution.py:237
  78.1 26.1 %all_to_all.15 = f32[128,1,128]{2,1,0:T(1,128)S(1)} all-to-all(f32[128,1,128]{2,1,0:T(1,128)S(1)} %broadcast_in_dim.9), channel_id=1, replica_groups=mesh['section'=8,'pair'=2,'core'=2,'far'=2,'depth'=8] {'section','far','..., dimensions={0} | all-to-all | bytes 131072 | tf_op jit(solution)/shard_map/all_to_all | solution.py:38
  104.2 0.7 shard_map.70
  (4 shorter events, 0.1 us)
Async XLA Ops:
  0.0 20.8 %collective-permute-start = (bf16[1728,128]{1,0:T(8,128)(2,1)}, bf16[1728,128]{1,0:T(8,128)(2,1)S(1)}, u32[]{:S(2)}, u32[]{:S(2)}) collective-permute-start(bf16[1728,128]{1,0:T(8,128)(2,1)} %bitcast.21), channel_id=1, source_target_pairs={{0,32},{32,0},{1,33},{33,1},{2,34},{34,2},{3,35},{35,3},{4,36},{36... | collective-permute-start | bytes 1327112 | tf_op jit(solution)/shard_map/ppermute | solution.py:30
  3.9 0.9 copy-start.4
  4.8 15.3 %copy-start = (bf16[1,64,5120]{2,1,0:T(8,128)(2,1)S(1)}, bf16[1,64,5120]{2,1,0:T(8,128)(2,1)}, u32[]{:S(2)}) copy-start(bf16[1,64,5120]{2,1,0:T(8,128)(2,1)} %param.6) | copy-start | bytes 1966084
  4.8 15.3 %copy-start.1 = (bf16[1,128,1728]{1,2,0:T(8,128)(2,1)S(1)}, bf16[1,128,1728]{1,2,0:T(8,128)(2,1)}, u32[]{:S(2)}) copy-start(bf16[1,128,1728]{1,2,0:T(8,128)(2,1)} %param.9) | copy-start | bytes 1327108
  5.8 29.7 %copy-start.3 = (s32[8]{0:T(128)S(1)}, s32[8]{0:T(128)}, u32[]{:S(2)}) copy-start(s32[8]{0:T(128)} %lens.3) | copy-start | bytes 100
  5.8 40.5 %all-to-all-start = ((bf16[64,8,640]{2,1,0:T(8,128)(2,1)}), bf16[64,8,640]{2,1,0:T(8,128)(2,1)S(1)}, u32[]{:S(2)}, u32[]{:S(2)}) async-start(bf16[64,8,640]{2,1,0:T(8,128)(2,1)} %shard_map.67), calls=%async_computation | async-start | bytes 1310720 | tf_op jit(solution)/shard_map/all_to_all | solution.py:38
  20.8 4.3 %collective-permute-start.1 = (bf16[3008,128]{1,0:T(8,128)(2,1)S(1)}, bf16[3008,128]{1,0:T(8,128)(2,1)S(1)}, u32[]{:S(2)}, u32[]{:S(2)}) collective-permute-start(bf16[3008,128]{1,0:T(8,128)(2,1)S(1)} %shard_map.64), channel_id=1, source_target_pairs={{0,16},{16,0},{1,17},{17,1},{2,18},{18,2},{3,19},{19,3},{4,20},{20... | collective-permute-start | bytes 2310152 | tf_op jit(solution)/shard_map/ppermute | solution.py:30
  23.1 12.4 %collective-permute-start.2 = (bf16[1728,128]{1,0:T(8,128)(2,1)S(1)}, bf16[1728,128]{1,0:T(8,128)(2,1)S(1)}, u32[]{:S(2)}, u32[]{:S(2)}) collective-permute-start(bf16[1728,128]{1,0:T(8,128)(2,1)S(1)} %collective-permute-done.across), channel_id=1, source_target_pairs={{0,16},{16,0},{1,17},{17,1},{2,18},{18,2},{3,19},{19,3},{4,20},{20... | collective-permute-start | bytes 1327112 | tf_op jit(solution)/shard_map/ppermute | solution.py:30
  25.8 16.0 %collective-permute-start.3 = (bf16[2,64,640]{2,1,0:T(8,128)(2,1)S(1)}, bf16[2,64,640]{2,1,0:T(8,128)(2,1)S(1)}, u32[]{:S(2)}, u32[]{:S(2)}) collective-permute-start(bf16[2,64,640]{2,1,0:T(8,128)(2,1)S(1)} %get-tuple-element.26), channel_id=1, source_target_pairs={{0,32},{32,0},{1,33},{33,1},{2,34},{34,2},{3,35},{35,3},{4,36},{36... | collective-permute-start | bytes 491528 | tf_op jit(solution)/shard_map/ppermute | solution.py:30
  29.2 13.6 %collective-permute-start.4 = (bf16[2,64,640]{2,1,0:T(8,128)(2,1)S(1)}, bf16[2,64,640]{2,1,0:T(8,128)(2,1)S(1)}, u32[]{:S(2)}, u32[]{:S(2)}) collective-permute-start(bf16[2,64,640]{2,1,0:T(8,128)(2,1)S(1)} %get-tuple-element.27), channel_id=1, source_target_pairs={{0,8},{8,0},{1,9},{9,1},{2,10},{10,2},{3,11},{11,3},{4,12},{12,4},... | collective-permute-start | bytes 491528 | tf_op jit(solution)/shard_map/ppermute | solution.py:30
  33.5 12.8 %collective-permute-start.5 = (bf16[2,64,640]{2,1,0:T(8,128)(2,1)S(1)}, bf16[2,64,640]{2,1,0:T(8,128)(2,1)S(1)}, u32[]{:S(2)}, u32[]{:S(2)}) collective-permute-start(bf16[2,64,640]{2,1,0:T(8,128)(2,1)S(1)} %get-tuple-element.28), channel_id=1, source_target_pairs={{0,40},{8,32},{32,8},{40,0},{1,41},{9,33},{33,9},{41,1},{2,42},{10... | collective-permute-start | bytes 491528 | tf_op jit(solution)/shard_map/ppermute | solution.py:34
  41.8 35.0 %copy-start.2 = (s32[1,1024]{1,0:T(1,128)S(1)}, s32[1,1024]{1,0:T(1,128)}, u32[]{:S(2)}) copy-start(s32[1,1024]{1,0:T(1,128)} %ids.1) | copy-start | bytes 12292
  47.9 28.9 %all-to-all-start.1 = ((s16[8,2,64,384]{3,2,1,0:T(8,128)(2,1)}), s16[8,2,64,384]{3,2,1,0:T(8,128)(2,1)S(1)}, u32[]{:S(2)}, u32[]{:S(2)}) async-start(s16[8,2,64,384]{3,2,1,0:T(8,128)(2,1)} %get-tuple-element.37), calls=%async_computation.1 | async-start | bytes 1572864 | tf_op jit(solution)/shard_map/all_to_all | solution.py:38
  53.3 4.0 %collective-permute-start.6 = (f32[2,2,64,384]{3,2,0,1:T(8,128)S(1)}, f32[2,2,64,384]{3,2,0,1:T(8,128)S(1)}, u32[]{:S(2)}, u32[]{:S(2)}) collective-permute-start(f32[2,2,64,384]{3,2,0,1:T(8,128)S(1)} %copy.9), channel_id=1, source_target_pairs={{0,16},{16,0},{1,17},{17,1},{2,18},{18,2},{3,19},{19,3},{4,20},{20... | collective-permute-start | bytes 1179656 | tf_op jit(solution)/shard_map/ppermute | solution.py:30
  57.3 9.6 %collective-permute-start.7 = (f32[2,64,384]{2,1,0:T(8,128)S(1)}, f32[2,64,384]{2,1,0:T(8,128)S(1)}, u32[]{:S(2)}, u32[]{:S(2)}) collective-permute-start(f32[2,64,384]{2,1,0:T(8,128)S(1)} %get-tuple-element.39), channel_id=1, source_target_pairs={{0,32},{32,0},{1,33},{33,1},{2,34},{34,2},{3,35},{35,3},{4,36},{36... | collective-permute-start | bytes 589832 | tf_op jit(solution)/shard_map/ppermute | solution.py:30
  59.2 10.7 %collective-permute-start.8 = (f32[2,64,384]{2,1,0:T(8,128)S(1)}, f32[2,64,384]{2,1,0:T(8,128)S(1)}, u32[]{:S(2)}, u32[]{:S(2)}) collective-permute-start(f32[2,64,384]{2,1,0:T(8,128)S(1)} %get-tuple-element.40.own), channel_id=1, source_target_pairs={{0,8},{8,0},{1,9},{9,1},{2,10},{10,2},{3,11},{11,3},{4,12},{12,4},... | collective-permute-start | bytes 589832 | tf_op jit(solution)/shard_map/ppermute | solution.py:30
  63.0 11.8 %collective-permute-start.9 = (f32[2,64,384]{2,1,0:T(8,128)S(1)}, f32[2,64,384]{2,1,0:T(8,128)S(1)}, u32[]{:S(2)}, u32[]{:S(2)}) collective-permute-start(f32[2,64,384]{2,1,0:T(8,128)S(1)} %get-tuple-element.39), channel_id=1, source_target_pairs={{0,40},{8,32},{32,8},{40,0},{1,41},{9,33},{33,9},{41,1},{2,42},{10... | collective-permute-start | bytes 589832 | tf_op jit(solution)/shard_map/ppermute | solution.py:34
